TPU v7x, 256 devices: a whole 4x4x8 slice. The times are simulated.
256 devices in a mesh: section: 64 (over z, y_lo, x), head: 4 (over y_hi, core).
Axes of the slice: x: 4, y: 4 (y_hi: 2, y_lo: 2; y = y_hi * 2 + y_lo), z: 8, core: 2. Of those that a mesh axis runs over, the one named last changes fastest.
Arguments:
- entering_hidden: bfloat16 [64, 128, 1792], P('section', None, 'head'), may hold values from -6 to 6
- entering_embed: bfloat16 [64, 128, 1792], P('section', None, 'head'), may hold values from -6 to 6
- incoming_embed: bfloat16 [1, 128, 1792], P(None, None, 'head'), may hold values from -6 to 6
- mixer_input_weight: bfloat16 [64, 1792, 3584], P('section', None, 'head'), may hold values from -0.125 to 0.125
- input_output_matrix_weight: bfloat16 [64, 1792, 128], P('section'), may hold values from -0.125 to 0.125
- step_size_weight: bfloat16 [64, 1792, 56], P('section', None, 'head'), may hold values from -0.125 to 0.125
- mixer_output_weight: bfloat16 [64, 3584, 1792], P('section', 'head'), may hold values from -0.09375 to 0.09375
- log_decay_rate: float32 [64, 56], P('section', 'head'), may hold values from -5 to 0
- step_size_bias: float32 [64, 56], P('section', 'head'), may hold values from -4 to -1
- skip_weight: float32 [64, 56], P('section', 'head'), may hold values from 0.5 to 1.5
- shared_query_key_value: bfloat16 [3584, 3, 3584], P('section', None, 'head'), may hold values from -6 to 6
- shared_output_weight: bfloat16 [1792, 3584], P('section', 'head'), may hold values from -0.09375 to 0.09375
- adapter_down: bfloat16 [64, 3584, 128], P('section'), may hold values from -0.09375 to 0.09375
- adapter_upward: bfloat16 [64, 128, 3, 3584], P('section', None, None, 'head'), may hold values from -0.5 to 0.5
- calls: int32 [64], P('section'), may hold values from 0 to 1, as said below
Outputs:
- section_outputs: bfloat16 [2, 64, 128, 1792], P(None, 'section', None, 'head')
Inputs may be any that keep to these rules, and one draw needn't show every extreme that they name: `calls`: the calling sections are every third section, starting at one of sections 0, 1 and 2; all others hold 0.
All inputs are finite; a program needn't handle non-finite values.
Results may differ from a plain program's by a relative error of at most 0.018.
Values may be sent and summed in bfloat16 or wider, within the bound.
A program may use at most 128 MiB of HBM per device.

v0:
```python
import jax
import jax.numpy as jnp
from jax import lax
from jax.sharding import PartitionSpec as P

P_SIZE = 64
N = 64
HEAD_WIDTH = 224
ROUNDS = 2


def shifted(block, axis, distance):
    devices = range(lax.axis_size(axis))
    route = [(i - distance, i) for i in devices if i - distance in devices]
    return lax.ppermute(block, axis, route)


def normed(values):
    return values * lax.rsqrt(jnp.mean(values * values, axis=-1, keepdims=True) + 1e-05)


def attend(query, keys, values):
    length = query.shape[0]
    heads = query.shape[1] // HEAD_WIDTH
    query = query.reshape(length, heads, HEAD_WIDTH)
    keys = keys.reshape(length, heads, HEAD_WIDTH)
    values = values.reshape(length, heads, HEAD_WIDTH)
    scores = jnp.einsum(
        "qhd,khd->hqk", query, keys, preferred_element_type=jnp.float32
    ) * HEAD_WIDTH ** (-0.5)
    causal = jnp.arange(length)[:, None] >= jnp.arange(length)[None, :]
    scores = jnp.where(causal[None], scores, -1e30)
    top = jnp.max(scores, axis=-1, keepdims=True)
    expd = jnp.exp(scores - top)
    probs = (expd / jnp.sum(expd, axis=-1, keepdims=True)).astype(jnp.bfloat16)
    mixed = jnp.einsum("hqk,khd->qhd", probs, values, preferred_element_type=jnp.float32)
    return mixed.reshape(length, heads * HEAD_WIDTH).astype(jnp.bfloat16)


def scan_mix(inputs, bmat, cmat, steps, log_decay_rate, skip_weight):
    length = inputs.shape[0]
    heads = steps.shape[1]
    rate = steps * jnp.exp(log_decay_rate)[None, :]
    total = jnp.cumsum(rate, axis=0).T
    causal = jnp.arange(length)[:, None] >= jnp.arange(length)[None, :]
    gap = jnp.where(causal[None], total[:, :, None] - total[:, None, :], 0.0)
    decay = jnp.where(causal[None], jnp.exp(-gap), 0.0)
    inner = jnp.dot(cmat, bmat.T, precision=lax.Precision.HIGHEST)
    mixing = inner[None] * decay * steps.T[:, None, :]
    split_in = inputs.reshape(length, heads, P_SIZE)
    out = jnp.einsum("htj,jhp->thp", mixing, split_in, precision=lax.Precision.HIGHEST)
    out = out + skip_weight[None, :, None] * split_in
    return out.reshape(length, heads * P_SIZE).astype(jnp.bfloat16)


def on_device(
    entering_hidden,
    entering_embed,
    incoming_embed,
    mixer_input_weight,
    input_output_matrix_weight,
    step_size_weight,
    mixer_output_weight,
    log_decay_rate,
    step_size_bias,
    skip_weight,
    shared_query_key_value,
    shared_output_weight,
    adapter_down,
    adapter_upward,
    calls,
):
    width = entering_hidden.shape[2]
    owned_columns = shared_query_key_value.shape[2]
    head_pos = lax.axis_index("head")
    first = lax.axis_index("section") == 0
    marker_value = calls[0].astype(jnp.float32)
    whole_qkv, whole_out = (
        lax.all_gather(shared_query_key_value, "section", axis=0, tiled=True),
        lax.all_gather(shared_output_weight, "section", axis=0, tiled=True),
    )
    flat_qkv = whole_qkv.reshape(whole_qkv.shape[0], 3 * owned_columns)
    hidden_rows = entering_hidden[0]
    embed_rows = entering_embed[0]
    results = []
    for rnd in range(ROUNDS):
        full_hidden, full_embed = (
            lax.all_gather(hidden_rows, "head", axis=1, tiled=True),
            lax.all_gather(embed_rows, "head", axis=1, tiled=True),
        )
        joined = jnp.concatenate([full_hidden, full_embed], axis=1).astype(jnp.float32)
        gate_values = normed(joined).astype(jnp.bfloat16)
        projected_rows = jnp.dot(gate_values, flat_qkv, preferred_element_type=jnp.float32)
        lowrank_update = jnp.dot(
            gate_values, adapter_down[0], preferred_element_type=jnp.float32
        ).astype(jnp.bfloat16)
        projected_rows = projected_rows + jnp.dot(
            lowrank_update,
            adapter_upward[0].reshape(adapter_upward.shape[1], 3 * owned_columns),
            preferred_element_type=jnp.float32,
        )
        projected_rows = projected_rows.reshape(gate_values.shape[0], 3, owned_columns).astype(
            jnp.bfloat16
        )
        mixed = attend(projected_rows[:, 0], projected_rows[:, 1], projected_rows[:, 2])
        attn = lax.dot_general(
            mixed, whole_out, (((1,), (1,)), ((), ())), preferred_element_type=jnp.float32
        )
        attn = lax.psum(attn, "head")
        middle_full = (full_hidden.astype(jnp.float32) + marker_value * attn).astype(jnp.bfloat16)
        middle_local = lax.dynamic_slice_in_dim(middle_full, head_pos * width, width, 1)
        unit = normed(middle_full.astype(jnp.float32)).astype(jnp.bfloat16)
        inputs = jax.nn.silu(
            jnp.dot(unit, mixer_input_weight[0], preferred_element_type=jnp.float32)
        )
        states = jax.nn.silu(
            jnp.dot(unit, input_output_matrix_weight[0], preferred_element_type=jnp.float32)
        )
        steps = jax.nn.softplus(
            jnp.dot(unit, step_size_weight[0], preferred_element_type=jnp.float32)
            + step_size_bias[0][None, :]
        )
        mixed_ssm = scan_mix(
            inputs, states[:, :N], states[:, N:], steps, log_decay_rate[0], skip_weight[0]
        )
        partial_out = jnp.dot(mixed_ssm, mixer_output_weight[0], preferred_element_type=jnp.float32)
        out_local = lax.psum_scatter(partial_out, "head", scatter_dimension=1, tiled=True)
        result = (middle_local.astype(jnp.float32) + out_local).astype(jnp.bfloat16)
        results.append(result)
        if rnd + 1 < ROUNDS:
            got_hidden, got_embed = shifted((result, embed_rows), "section", 1)
            fresh = incoming_embed[rnd]
            hidden_rows = jnp.where(first, fresh, got_hidden)
            embed_rows = jnp.where(first, fresh, got_embed)
    return jnp.stack(results, axis=0)[:, None]


def solution(mesh):
    in_specs = (
        P("section", None, "head"),
        P("section", None, "head"),
        P(None, None, "head"),
        P("section", None, "head"),
        P("section", None, None),
        P("section", None, "head"),
        P("section", "head", None),
        P("section", "head"),
        P("section", "head"),
        P("section", "head"),
        P("section", None, "head"),
        P("section", "head"),
        P("section", None, None),
        P("section", None, None, "head"),
        P("section"),
    )
    out_specs = P(None, "section", None, "head")
    return jax.shard_map(
        on_device, mesh=mesh, in_specs=in_specs, out_specs=out_specs, check_vma=False
    )
```

profile of v0, /device:TPU:1, one launch (start us, length us, event | category | flops | bytes accessed | tf_op | source)
XLA Modules:
  0.0 977.0 jit_solution(9398217936215603877)
XLA Ops:
  6.5 0.7 all-gather.8.cloned.1.call-update
  7.3 0.7 all-gather.6.cloned.1.call-update
  8.1 11.6 %all-gather.1 = bf16[1,128,1792]{1,2,0:T(8,128)(2,1)} all-gather(bf16[1,128,448]{1,2,0:T(8,128)(2,1)} %param.16), channel_id=3, replica_groups=mesh['section'=64,'head'=4] {'head'}, dimensions={2}, use_global_device_ids=true | all-gather | bytes 573440 | tf_op jit(solution)/shard_map/all_gather | solution.py:89
  19.6 2.0 copy.65
  21.6 8.9 all-gather
  30.5 2.0 copy.64
  32.5 2.3 copy.67
  34.8 1.4 fusion.18
  36.2 236.2 %all-gather.8.cloned.1.call-done = bf16[64,28,896]{2,1,0:T(8,128)(2,1)} async-done(((bf16[1,28,896]{2,1,0:T(8,128)(2,1)}), bf16[64,28,896]{2,1,0:T(8,128)(2,1)}) %all-gather.8.cloned.1.call-update) | async-done | bytes 3211280 | tf_op jit(solution)/shard_map/all_gather | solution.py:80
  272.4 6.0 reshape.85
  278.4 335.7 %all-gather.6.cloned.1.call-done = bf16[3584,3,896]{2,0,1:T(8,128)(2,1)} async-done(((bf16[56,3,896]{2,0,1:T(8,128)(2,1)}), bf16[3584,3,896]{2,0,1:T(8,128)(2,1)}) %all-gather.6.cloned.1.call-update) | async-done | bytes 19267600 | tf_op jit(solution)/shard_map/all_gather | solution.py:79
  614.1 25.6 %copy.66 = bf16[3584,3,896]{0,2,1:T(8,128)(2,1)} copy(bf16[3584,3,896]{2,0,1:T(8,128)(2,1)} %all-gather.6.cloned.1.call-done) | data formatting | bytes 38535168 | tf_op jit(solution)/shard_map/all_gather | solution.py:79
  639.6 14.2 %fusion.89 = f32[128,2688]{1,0:T(8,128)} fusion(bf16[3584,2688]{0,1:T(8,128)(2,1)} %bitcast.156, f32[128]{0:T(128)S(1)} %add_rsqrt_fusion.3, bf16[128,1792]{1,0:T(8,128)(2,1)} %bitcast.162, bf16[128,1792]{1,0:T(8,128)(2,1)} %bitcast.159), kind=kOutput, calls=%fused_computation.106 | convolution fusion | flops 2469003264 | bytes 21561856 | tf_op jit(solution)/shard_map/dot_general | solution.py:93
  653.8 3.7 fusion.2
  657.5 2.2 copy.68
  659.7 1.9 fusion.124
  661.6 0.3 fusion.29
  662.0 1.9 convolution_convert_fusion.1
  663.9 4.0 fusion.127
  668.9 83.5 %all-reduce.3.cloned.1.call-done = f32[128,1792]{1,0:T(8,128)} async-done(((f32[128,1792]{1,0:T(8,128)}), f32[128,1792]{1,0:T(8,128)}) %all-reduce.3.cloned.1.call-update) | async-done | bytes 917520 | tf_op jit(solution)/shard_map/psum | solution.py:109
  752.4 1.5 fusion.32
  754.0 0.8 copy-done.2
  754.8 3.4 divide_multiply_fusion.1
  758.2 2.0 copy.70
  760.2 1.4 compare_select_fusion.2
  762.0 1.6 divide_multiply_fusion.3
  763.6 0.3 fusion.94
  763.9 3.1 fusion.26
  767.0 2.3 fusion.12
  769.4 0.8 copy.79
  770.2 3.7 collective-permute-start.1
  773.9 30.9 %reduce-scatter.7.cloned.1.call-done = f32[448,128]{1,0:T(8,128)} async-done(((f32[1792,128]{1,0:T(8,128)}), f32[448,128]{1,0:T(8,128)}) %reduce-scatter.7.cloned.1.call-update) | async-done | bytes 229392
  804.9 1.1 copy.94
  805.9 1.7 add_convert_fusion.3
  807.6 3.7 collective-permute-start
  811.4 1.0 copy.76
  812.4 0.8 collective-permute-done
  813.2 0.7 bitcast_select_fusion.1
  813.8 1.0 copy.80
  814.9 9.7 all_gather.23
  824.7 8.7 all_gather.22
  833.3 0.8 copy-done.1
  834.1 1.5 fusion.20
  835.6 14.1 %fusion.56 = f32[128,2688]{1,0:T(8,128)} fusion(bf16[3584,2688]{0,1:T(8,128)(2,1)} %bitcast.157, f32[128]{0:T(128)S(1)} %add_rsqrt_fusion.1, bf16[128,1792]{0,1:T(8,128)(2,1)} %all_gather.23, bf16[128,1792]{0,1:T(8,128)(2,1)} %copy-done.1), kind=kOutput, calls=%fused_computation.72 | convolution fusion | flops 2469003264 | bytes 21561856 | tf_op jit(solution)/shard_map/dot_general | solution.py:93
  849.7 3.7 fusion.3
  853.4 2.2 copy.81
  855.7 1.9 fusion.123
  857.9 1.9 convolution_convert_fusion
  859.8 4.0 fusion.128
  863.9 2.0 copy.78
  865.9 50.8 %all-reduce.5.cloned.1.call-done = f32[128,1792]{1,0:T(8,128)} async-done(((f32[128,1792]{1,0:T(8,128)}), f32[128,1792]{1,0:T(8,128)}) %all-reduce.5.cloned.1.call-update) | async-done | bytes 917520 | tf_op jit(solution)/shard_map/psum | solution.py:109
  916.6 1.5 fusion.34
  918.2 3.6 divide_multiply_fusion
  921.8 0.3 compare_select_fusion
  922.2 0.4 divide_multiply_fusion.2
  922.6 2.0 copy.83
  925.0 0.3 fusion.91
  925.3 3.1 fusion.27
  928.4 2.3 fusion.15
  930.7 35.5 %reduce-scatter.9.cloned.1.call-done = f32[448,128]{1,0:T(8,128)} async-done(((f32[1792,128]{1,0:T(8,128)}), f32[448,128]{1,0:T(8,128)}) %reduce-scatter.9.cloned.1.call-update) | async-done | bytes 229392
  966.2 1.1 copy.96
  967.3 1.0 fusion.78
  968.4 0.9 maximum_bitcast_fusion
  969.3 0.8 copy.88
  (52 shorter events, 2.1 us)
Async XLA Ops:
  6.5 760.5 %copy-start = (bf16[1,896,1792]{2,1,0:T(8,128)(2,1)S(1)}, bf16[1,896,1792]{2,1,0:T(8,128)(2,1)}, u32[]{:S(2)}) copy-start(bf16[1,896,1792]{2,1,0:T(8,128)(2,1)} %param.21) | copy-start | bytes 9633796
  6.5 15.1 %copy-start.5 = (bf16[1,128,448]{1,2,0:T(8,128)(2,1)S(1)}, bf16[1,128,448]{1,2,0:T(8,128)(2,1)}, u32[]{:S(2)}) copy-start(bf16[1,128,448]{1,2,0:T(8,128)(2,1)} %param.15) | copy-start | bytes 344068
  6.5 265.9 %all-gather.8.cloned.1.call-start = ((), (), s32[]{:S(2)}) async-start(), calls=%async_computation.5 | async-start | bytes 3727360 | tf_op jit(solution)/shard_map/all_gather | solution.py:80
  7.3 606.8 %all-gather.6.cloned.1.call-start = ((), (), s32[]{:S(2)}) async-start(), calls=%async_computation.2 | async-start | bytes 19568640 | tf_op jit(solution)/shard_map/all_gather | solution.py:79
  8.0 744.4 %all-reduce.3.cloned.1.call-start = ((), (), s32[]{:S(2)}) async-start(), calls=%async_computation.3 | async-start | bytes 1835008 | tf_op jit(solution)/shard_map/psum | solution.py:109
  663.9 5.1 copy-start.9
  667.9 137.0 %reduce-scatter.7.cloned.1.call-start = ((), (), s32[]{:S(2)}) async-start(), calls=%async_computation.6 | async-start | bytes 1146880
  754.0 0.8 copy-start.2
  754.8 5.4 copy-start.7
  754.8 5.4 copy-start.10
  758.2 5.7 copy-start.11
  767.0 2.4 copy-start.4
  769.4 147.3 %all-reduce.5.cloned.1.call-start = ((), (), s32[]{:S(2)}) async-start(), calls=%async_computation.4 | async-start | bytes 1835008 | tf_op jit(solution)/shard_map/psum | solution.py:109
  770.2 42.2 %collective-permute-start.1 = (bf16[128,448]{1,0:T(8,128)(2,1)}, bf16[128,448]{1,0:T(8,128)(2,1)}, u32[]{:S(2)}, u32[]{:S(2)}) collective-permute-start(bf16[128,448]{1,0:T(8,128)(2,1)} %bitcast.27), channel_id=1, source_target_pairs={{0,4},{4,8},{8,12},{12,16},{16,20},{20,24},{24,28},{28,32},{32,36}... | collective-permute-start | bytes 344072 | tf_op jit(solution)/shard_map/ppermute | solution.py:15
  807.6 5.5 collective-permute-start
  833.3 0.8 copy-start.1
  863.8 102.4 %reduce-scatter.9.cloned.1.call-start = ((), (), s32[]{:S(2)}) async-start(), calls=%async_computation.7 | async-start | bytes 1146880
  918.2 4.0 copy-start.3
  918.2 3.6 copy-start.8
  918.2 4.0 copy-start.6
Sparse Core Ops, SparseCore 0:
  9.2 263.2 all-gather.7
  274.2 339.8 all-gather.5
  668.0 84.3 all-reduce.2
  769.5 35.3 reduce-scatter.6
  863.9 52.6 all-reduce.4
  930.9 35.3 reduce-scatter.8
where the time goes:
time: 979 us; the launch traced here: 977 us
  waiting for transfers between devices  775 us (79%)
  matrix products  70.1 us (7%)
  local copies, waits for them, and re-layouts  60.1 us (6%)
  blocking collectives  38.8 us (4%)
  between operations  14.4 us (1%)
  other arithmetic  11 us (1%)
    all_gather x1, waiting for transfers between devices, on_device(): lax.all_gather(shared_query_key_value, 'section', axis=0, tiled=True)  336 us
    all_gather x1, waiting for transfers between devices, on_device(): lax.all_gather(shared_output_weight, 'section', axis=0, tiled=True)  236 us
    psum x2, waiting for transfers between devices, on_device(): attn = lax.psum(attn, 'head')  134 us
    unnamed x8, waiting for transfers between devices  67.9 us
    dot_general x2, matrix products, on_device(): jnp.dot(gate_values, flat_qkv, preferred_element_type=jnp.float32)  28.3 us
    all_gather x1, local copies, waits for them, and re-layouts, on_device(): lax.all_gather(shared_query_key_value, 'section', axis=0, tiled=True)  25.6 us
    all_gather x2, blocking collectives, on_device(): lax.all_gather(embed_rows, 'head', axis=1, tiled=True)  21.2 us
  transfers between devices with their start and end apart: 8, of which 7 were waited for; matrix products, arithmetic and copies ran while one was open for 2% of the time, Pallas kernels for 0%

commit v1 on v0

v1 whole, which is shorter than its diff:
```python
import jax
import jax.numpy as jnp
from jax import lax
from jax.experimental import pallas as pl
from jax.experimental.pallas import tpu as pltpu
from jax.sharding import PartitionSpec as P

MESH = pl.DeviceIdType.MESH
BF = jnp.bfloat16
F32 = jnp.float32
NT = (((1,), (1,)), ((), ()))
TN = (((0,), (0,)), ((), ()))
HIGH = lax.Precision.HIGHEST
D = 1792
Q = 448
SEQ = 128
HEADS = 14
HEAD_WIDTH = 224
EPS = 1e-05
SENDS = 128


def iota(shape, dim):
    return lax.broadcasted_iota(jnp.int32, shape, dim)


def dot(a, b, dims=(((1,), (0,)), ((), ()))):
    return lax.dot_general(a, b, dims, preferred_element_type=F32)


def silu(v):
    return v / (1.0 + jnp.exp(-v))


def softplus(v):
    return jnp.maximum(v, 0.0) + jnp.log(1.0 + jnp.exp(-jnp.abs(v)))


def kernel(
    h0_in, e0_in, inc_in, wmix_in, wio_in, wdt_ref, wom_in, decay_ref, bias_ref, skip_ref,
    qkv_in, wo_ref, down_in, up_in, calls_ref,
    out_ref,
    xall, xs, wg, wmix, wio, wom, down, up, qw, sel, a2s, a2r, wo32, ups, upr, low, misc,
    acc, wog, mx, rs2s, rs2r, atb, atr, mid, hf, mbuf, ubuf, ybuf, xbuf, pbuf, cbuf, rss, rsr,
    outq, send_sem, recv_sem, load_sem,
):
    s = lax.axis_index("section")
    h = lax.axis_index("head")
    x = lax.rem(s, 4)
    y = lax.rem(s // 4, 2)
    z = s // 8
    core = lax.rem(h, 2)
    base = s - x
    sec_up = lax.rem(z + 1, 8) * 8 + lax.rem(s, 8)
    sec_down = lax.rem(z + 7, 8) * 8 + lax.rem(s, 8)
    sec_y = s + 4 - 8 * y
    sec_next = lax.rem(s + 1, 64)
    sec_prev = lax.rem(s + 63, 64)
    x_next = lax.rem(x + 1, 4)

    def line(j):
        return lax.rem(x + j, 4)

    def sib(j):
        return lax.rem(h + j, 4)

    index = {}
    descs = {}

    def remote(key, src, dst, section, head):
        at = index.setdefault(key, len(index))
        desc = pltpu.make_async_remote_copy(
            src_ref=src, dst_ref=dst, send_sem=send_sem.at[at], recv_sem=recv_sem.at[at],
            device_id={"section": section, "head": head}, device_id_type=MESH,
        )
        descs[key] = desc
        return desc

    def start(key, src, dst, section=None, head=None):
        remote(key, src, dst, s if section is None else section, h if head is None else head).start()

    def pass_on(key, src, dst):
        fresh = remote((key,), inc_in, dst, sec_next, h)
        usual = remote((key,), src, dst, sec_next, h)
        pl.when(s == 63)(lambda: fresh.start())
        pl.when(s != 63)(lambda: usual.start())

    def got(*key):
        descs[key].wait_recv()

    loads = {}

    def load(name, src, dst):
        loads[name] = pltpu.make_async_copy(src, dst, load_sem.at[len(loads)])
        loads[name].start()

    own = pl.ds(pl.multiple_of(h * Q, Q), Q)
    load("qkv", qkv_in, qw)
    load("h0", h0_in, xall.at[x, 0, own])
    load("e0", e0_in, xall.at[x, 1, own])
    load("down", down_in, down)
    load("up", up_in, up)
    load("wmix", wmix_in, wmix)
    load("wio", wio_in, wio)
    load("wom", wom_in, wom)

    barrier = pltpu.get_barrier_semaphore()
    peers = [(base + line(j), h) for j in (1, 2, 3)] + [(s, sib(j)) for j in (1, 2, 3)]
    peers += [(sec_up, h), (sec_down, h), (sec_y, h), (sec_next, h), (sec_prev, h)]
    for section, head in peers:
        pl.semaphore_signal(
            barrier, inc=1, device_id={"section": section, "head": head}, device_id_type=MESH
        )
    for i in range(4):
        r, c = iota((896, 256), 0), iota((896, 256), 1)
        sel[i] = jnp.where((r == c + 224 * i) & (c < 224), 1.0, 0.0).astype(BF)
    wo32[...] = jnp.zeros_like(wo32)
    wo32[0:28, :] = wo_ref[...]
    pl.semaphore_wait(barrier, len(peers))

    def gather_heads(name, src, dst_of):
        for j in (1, 2, 3):
            start((name, j), src, dst_of, None, sib(j))

    def wait_heads(name):
        for j in (1, 2, 3):
            got(name, j)

    gather_heads("h0", h0_in, xall.at[x, 0, own])
    gather_heads("e0", e0_in, xall.at[x, 1, own])

    pass_on("e1p", e0_in, xall.at[x_next, 3, own])

    loads["qkv"].wait()
    for i in range(4):
        for k in range(3):
            block = dot(qw[k], sel[i])
            block = jnp.concatenate([block, jnp.zeros((8, 256), F32)], axis=0)
            a2s[i, :, 256 * k : 256 * k + 256] = block.astype(BF)
    for j in (1, 2, 3):
        start(("a2a", j), a2s.at[line(j)], a2r.at[x], base + line(j))
    a2r[x] = a2s[x]
    for i in range(3):
        wg[z, y, 224:256, 256 * i : 256 * i + 256] = dot(wo32[...], sel[i]).astype(BF)
    last = dot(wo32[...], sel[3]).astype(BF)
    wg[z, y, 256:272, 0:256] = last[0:16]
    wg[z, y, 256:272, 256:512] = last[16:32]
    wg[z, y, 256:272, 512:768] = jnp.zeros((16, 256), BF)
    r, c = iota((224, 256), 0), iota((224, 256), 1)
    compact = jnp.where(((c - 8 * (c >> 6)) == r) & ((c & 63) < 56), 1.0, 0.0).astype(BF)
    for j in (1, 2, 3):
        got("a2a", j)
    packed = jnp.concatenate([a2r[0], a2r[1], a2r[2], a2r[3]], axis=0)
    wg[z, y, 0:224, :] = dot(compact, packed).astype(BF)

    halves = {None: (0, 272), 0: (0, 144), 1: (144, 128)}

    def piece(other, dz, half):
        first, rows = halves[half]
        return wg.at[lax.rem(z + dz + 8, 8), (1 - y) if other else y, pl.ds(first, rows)]

    def push(way, other, dz, half=None):
        ref = piece(other, dz, half)
        section = {"down": sec_down, "up": sec_up, "y": sec_y}[way]
        start((way, other, dz, half), ref, ref, section)

    def pump(step):
        if step == 0:
            push("down", 0, 0)
            push("up", 0, 0)
            push("y", 0, 0)
        if step == 1:
            got("down", 0, 0, None)
            push("down", 0, 1)
            push("y", 0, 1)
            got("up", 0, 0, None)
            push("up", 0, -1)
        if step == 2:
            got("down", 0, 1, None)
            push("down", 0, 2)
            push("y", 0, 2)
            got("up", 0, -1, None)
            push("up", 0, -2)
            push("y", 0, -2)
        if step == 3:
            got("down", 0, 2, None)
            push("down", 0, 3, 0)
            got("up", 0, -2, None)
            push("up", 0, -3, 1)
            push("y", 0, -1)
        if step == 4:
            got("y", 0, 0, None)
            got("y", 0, 1, None)
            got("y", 0, 2, None)
            push("down", 1, 2)
            got("y", 0, -2, None)
            push("up", 1, -2)
        if step == 5:
            got("down", 1, 2, None)
            push("down", 1, 3, 0)
            got("up", 1, -2, None)
            push("up", 1, -3, 1)
        if step == 6:
            got("y", 0, -1, None)
            got("down", 0, 3, 0)
            got("up", 0, -3, 1)
            got("down", 1, 3, 0)
            got("up", 1, -3, 1)

    pump(0)

    half_rows = pl.ds(pl.multiple_of(core * 896, 896), 896)
    twin = h + 1 - 2 * core

    def gather_line(n):
        for j in (1, 2, 3):
            ref = xall.at[x, n, half_rows]
            start(("line", n, j), ref, ref, base + line(j))

    def share_line(n):
        for j in (1, 2, 3):
            got("line", n, j)
            ref = xall.at[line(4 - j), n, half_rows]
            start(("twin", n, j), ref, ref, None, twin)

    def wait_share(n):
        for j in (1, 2, 3):
            got("twin", n, j)

    def row_scale(n):
        total = jnp.zeros((1, SEQ), F32)
        for part in (0, 1):
            def add(t, total):
                block = xall[x, 2 * n + part, pl.ds(pl.multiple_of(t * 128, 128), 128), :].astype(F32)
                return total + jnp.sum(block * block, axis=0, keepdims=True)
            total = lax.fori_loop(0, 14, add, total)
        return lax.rsqrt(total / (2 * D) + EPS)

    def make_low(n):
        scale = row_scale(n)
        total = jnp.zeros((128, SEQ), F32)
        for part in (0, 1):
            total = total + dot(down[part * D : part * D + D, :], xall[x, 2 * n + part], TN)
        low[x, n] = (total * scale).astype(BF)
        rows = iota((8, 128), 0)
        mark = calls_ref[0].astype(F32)
        misc[x, n] = jnp.where(rows == 0, scale, mark)
        for j in (1, 2, 3):
            start(("low", n, j), low.at[x, n], low.at[x, n], base + line(j))
            start(("misc", n, j), misc.at[x, n], misc.at[x, n], base + line(j))

    def wait_low(n):
        for j in (1, 2, 3):
            got("low", n, j)
            got("misc", n, j)

    loads["h0"].wait()
    loads["e0"].wait()
    wait_heads("h0")
    gather_line(0)
    wait_heads("e0")
    gather_line(1)
    got("e1p")
    gather_heads("e1", xall.at[x, 3, own], xall.at[x, 3, own])
    loads["down"].wait()
    loads["up"].wait()
    for i in range(4):
        for k in range(3):
            ups[i, :, 256 * k : 256 * k + 256] = dot(up[k], sel[i]).astype(BF)
    for j in (1, 2, 3):
        start(("up", j), ups.at[line(j)], upr.at[x], base + line(j))
    upr[x] = ups[x]
    make_low(0)
    wait_heads("e1")
    gather_line(3)
    pump(1)

    def eye_column(row, size):
        r, c = iota((size, size), 0), iota((size, size), 1)
        return jnp.sum(jnp.where(r == c, row, 0.0), axis=1, keepdims=True)

    def mixer_in(n, src):
        def add(t, total):
            block = src[pl.ds(pl.multiple_of(t * 128, 128), 128), :].astype(F32)
            return total + jnp.sum(block * block, axis=0, keepdims=True)
        total = lax.fori_loop(0, 14, add, jnp.zeros((1, SEQ), F32))
        scale = lax.rsqrt(total / D + EPS)
        for t in range(14):
            block = src[128 * t : 128 * t + 128, :].astype(F32) * scale
            ubuf[:, 128 * t : 128 * t + 128] = block.T.astype(BF)

        def columns(t, carry):
            at = pl.ds(pl.multiple_of(t * 256, 256), 256)
            xbuf[:, at] = silu(dot(ubuf[...], wmix[:, at]))
            return carry
        lax.fori_loop(0, 3, columns, 0)
        xbuf[:, 768:896] = silu(dot(ubuf[...], wmix[:, 768:896]))

    def mixer_out(n):
        bc = silu(dot(ubuf[...], wio[...]))
        bias = eye_column(bias_ref[...], HEADS)
        rate = jnp.exp(eye_column(decay_ref[...], HEADS))
        dt = softplus(dot(wdt_ref[...], ubuf[...], NT) + bias)
        upper = jnp.where(iota((128, 128), 0) <= iota((128, 128), 1), 1.0, 0.0)
        cum = lax.dot_general(
            dt * rate, upper, (((1,), (0,)), ((), ())), precision=HIGH, preferred_element_type=F32
        )
        cbuf[...] = jnp.zeros_like(cbuf)
        cbuf[0:HEADS, :] = cum
        cum_t = cbuf[...].T
        lanes = iota((128, 128), 1)
        rolled = pltpu.roll(bc, 64, axis=1)
        inner = lax.dot_general(
            jnp.where(lanes < 64, rolled, 0.0), jnp.where(lanes < 64, bc, 0.0), NT,
            precision=HIGH, preferred_element_type=F32,
        )
        causal = iota((128, 128), 0) >= lanes
        for pair in range(HEADS // 2):
            mixes = []
            for j in (2 * pair, 2 * pair + 1):
                gap = jnp.where(causal, cum[j : j + 1, :] - cum_t[:, j : j + 1], -1e30)
                mixes.append((inner * jnp.exp(gap) * dt[j : j + 1, :]).astype(BF))
            block = xbuf[:, 128 * pair : 128 * pair + 128]
            both = dot(jnp.concatenate(mixes, axis=0), block.astype(BF))
            skip = jnp.where(lanes < 64, skip_ref[0, 2 * pair], skip_ref[0, 2 * pair + 1])
            mixed = jnp.where(lanes < 64, both[0:128], both[128:256]) + skip * block
            ybuf[:, 128 * pair : 128 * pair + 128] = mixed.astype(BF)

        def columns(t, carry):
            at = pl.ds(pl.multiple_of(t * 256, 256), 256)
            part = dot(ybuf[...], wom[:, at])
            pbuf[pl.ds(pl.multiple_of(t * 256, 256), 128), :] = part[:, 0:128].T
            pbuf[pl.ds(pl.multiple_of(t * 256 + 128, 128), 128), :] = part[:, 128:256].T
            return carry
        lax.fori_loop(0, 7, columns, 0)
        for j in (1, 2, 3):
            at = pl.ds(pl.multiple_of(sib(j) * Q, Q), Q)
            rss[n, j - 1] = pbuf[at, :].astype(BF)
            start(("rs", n, j), rss.at[n, j - 1], rsr.at[n, j - 1], None, sib(j))

    def mixer_sum(n, src):
        total = src[own, :].astype(F32) + pbuf[own, :]
        for j in (1, 2, 3):
            got("rs", n, j)
            total = total + rsr[n, j - 1].astype(F32)
        outq[n] = total.astype(BF)

    loads["wmix"].wait()
    loads["wio"].wait()
    loads["wom"].wait()
    mixer_in(0, xall.at[x, 0])
    share_line(0)
    share_line(1)
    pump(2)
    mixer_out(0)
    mixer_sum(0, xall.at[x, 0])

    pass_on("h1p", outq.at[0], xall.at[x_next, 2, own])

    wait_low(0)
    for j in (1, 2, 3):
        got("up", j)
    marks = [misc[c, 0, 1:2, :] for c in range(3)]
    marks_bf = [m.astype(BF) for m in marks]
    identity = jnp.where(iota((128, 128), 0) == iota((128, 128), 1), 1.0, 0.0).astype(BF)

    def pick(values, masks):
        return values[0] * masks[0] + values[1] * masks[1] + values[2] * masks[2]

    def spread(n):
        def body(t, carry):
            part = t // 8
            at = pl.ds(pl.multiple_of((t - 8 * part) * 224, 224), 224)
            first = pick([xall[c, 2 * n + part, at, :] for c in range(3)], marks_bf)
            xs[n, t, 0:128, :] = dot(identity, first, NT).astype(BF)
            xs[n, t, 128:256, :] = dot(identity, xall[3, 2 * n + part, at, :], NT).astype(BF)
            return carry
        lax.fori_loop(0, 16, body, 0)

    wait_share(0)
    wait_share(1)
    spread(0)
    pump(3)
    got("h1p")
    gather_heads("h1", xall.at[x, 2, own], xall.at[x, 2, own])
    share_line(3)

    def project(n, other, dz):
        zz, yy = lax.rem(z + dz + 8, 8), (1 - y) if other else y
        acc[n] += dot(xs[n, 2 * zz + yy], wg[zz, yy, 0:224, :])

    acc[0] = jnp.zeros((256, 768), F32)
    for dz in (0, 1, -1, 2, -2, 3, -3):
        project(0, 0, dz)
    pump(4)
    project(0, 1, 0)
    project(0, 1, 1)
    project(0, 1, 2)
    project(0, 1, -2)
    wait_heads("h1")
    gather_line(2)
    make_low(1)
    pump(5)
    project(0, 1, 3)
    project(0, 1, -3)
    pump(6)
    project(0, 1, -1)
    project(0, 0, 4)
    project(0, 1, 4)

    def attend(n):
        up_first = pick([upr[c] for c in range(3)], [m[:, 0:1] for m in marks_bf])
        low_first = pick([low[c, n] for c in range(3)], marks_bf)
        scale_first = pick([misc[c, n, 0:1, :] for c in range(3)], marks)
        causal = iota((128, 128), 0) >= iota((128, 128), 1)
        for slot in (0, 1):
            low_t = low_first if slot == 0 else low[3, n]
            up_slot = up_first if slot == 0 else upr[3]
            scale = eye_column(scale_first if slot == 0 else misc[3, n, 0:1, :], 128)
            rows = slice(128 * slot, 128 * slot + 128)
            proj = (acc[n, rows, :] * scale + dot(low_t, up_slot, TN)).astype(BF)
            query, keys, values = proj[:, 0:256], proj[:, 256:512], proj[:, 512:768]
            scores = dot(query, keys, NT) * HEAD_WIDTH ** (-0.5)
            scores = jnp.where(causal, scores, -1e30)
            expd = jnp.exp(scores - jnp.max(scores, axis=-1, keepdims=True))
            probs = (expd / jnp.sum(expd, axis=-1, keepdims=True)).astype(BF)
            mx[n, x, rows, :] = dot(probs, values).astype(BF)
        for j in (1, 2, 3):
            ref = mx.at[n, x]
            start(("mx", n, j), ref, ref, base + line(j))

    attend(0)

    def unpack(t, carry):
        zz = t // 2
        yy = t - 2 * zz
        at = pl.multiple_of(t * 32, 32)
        wog[pl.ds(at, 32), 0:768] = wg[zz, yy, 224:256, :]
        wog[pl.ds(at, 16), 768:1024] = wg[zz, yy, 256:272, 0:256]
        wog[pl.ds(at + 16, 16), 768:1024] = wg[zz, yy, 256:272, 256:512]
        return carry
    lax.fori_loop(0, 16, unpack, 0)

    pt = {}

    def out_project(n):
        for j in (1, 2, 3):
            got("mx", n, j)
        for q in range(4):
            rows = slice(128 * q, 128 * q + 128)
            total = dot(wog[rows, 0:256], mx[n, 0], NT)
            for i in (1, 2, 3):
                total = total + dot(wog[rows, 256 * i : 256 * i + 256], mx[n, i], NT)
            rs2s[n, q] = total.astype(BF)
        for j in (1, 2, 3):
            start(("rs2", n, j), rs2s.at[n, sib(j)], rs2r.at[n, j - 1], None, sib(j))

    def send_attn(n):
        total = rs2s[n, h].astype(F32)
        for j in (1, 2, 3):
            got("rs2", n, j)
            total = total + rs2r[n, j - 1].astype(F32)
        atb[n, 0] = total[:, 0:128].astype(BF)
        atb[n, 1] = total[:, 128:256].astype(BF)
        for j in (1, 2, 3):
            start(("at", n, j), atb.at[n, line(j) // 3], atr.at[n, x], base + line(j))
        atr[n, x] = atb[n, x // 3]

    def make_middle(n):
        for j in (1, 2, 3):
            got("at", n, j)
        r, c = iota((224, 256), 0), iota((224, 256), 1)
        home = (4 * ((c >> 5) & 1) + (c >> 6)) * 28 + (c & 31)
        order = jnp.where((r == home) & ((c & 31) < 28), 1.0, 0.0).astype(BF)
        for half in (0, 1):
            stack = jnp.concatenate([atr[n, i, 64 * half : 64 * half + 64, :] for i in range(4)], axis=0)
            at = pl.ds(pl.multiple_of(h * Q + 224 * half, 224), 224)
            mid[n, at, :] = (xall[x, 2 * n, at, :].astype(F32) + dot(order, stack)).astype(BF)
        gather_heads(("mid", n), mid.at[n, own], mid.at[n, own])

    mark_here = calls_ref[0].astype(F32)

    def choose(n, plain):
        wait_heads(("mid", n))

        def body(t, carry):
            at = pl.ds(pl.multiple_of(t * 128, 128), 128)
            called = mid[n, at, :].astype(F32)
            mbuf[n, at, :] = (called * mark_here + plain[at, :].astype(F32) * (1.0 - mark_here)).astype(BF)
            return carry
        lax.fori_loop(0, 14, body, 0)

    share_line(2)
    out_project(0)
    wait_share(3)
    wait_share(2)
    wait_low(1)
    send_attn(0)
    spread(1)
    make_middle(0)
    acc[1] = jnp.zeros((256, 768), F32)

    def project_all(t, carry):
        zz = t // 2
        acc[1] += dot(xs[1, t], wg[zz, t - 2 * zz, 0:224, :])
        return carry
    lax.fori_loop(0, 16, project_all, 0)
    attend(1)
    choose(0, xall.at[x, 0])
    mixer_in(1, mbuf.at[0])
    mixer_out(1)
    out_project(1)
    mixer_sum(1, mbuf.at[0])

    pass_on("hfp", outq.at[1], hf.at[own])

    save0 = pltpu.make_async_copy(outq.at[1], out_ref.at[0], load_sem.at[10])
    save0.start()
    send_attn(1)
    make_middle(1)
    got("hfp")
    gather_heads("hf", hf.at[own], hf.at[own])
    wait_heads("hf")
    choose(1, hf)
    mixer_in(2, mbuf.at[1])
    mixer_out(2)
    mixer_sum(2, mbuf.at[1])
    save1 = pltpu.make_async_copy(outq.at[2], out_ref.at[1], load_sem.at[11])
    save1.start()
    for desc in descs.values():
        desc.wait_send()
    save0.wait()
    save1.wait()


def on_device(
    entering_hidden, entering_embed, incoming_embed, mixer_input_weight,
    input_output_matrix_weight, step_size_weight, mixer_output_weight, log_decay_rate,
    step_size_bias, skip_weight, shared_query_key_value, shared_output_weight, adapter_down,
    adapter_upward, calls,
):
    flip = lambda v: jnp.swapaxes(v, 1, 2)[0]
    hbm = pl.BlockSpec(memory_space=pl.ANY)
    vmem = pl.BlockSpec(memory_space=pltpu.VMEM)
    smem = pl.BlockSpec(memory_space=pltpu.SMEM)
    scratch = [
        ((4, 4, D, SEQ), BF),
        ((2, 16, 256, 224), BF),
        ((8, 2, 272, 768), BF),
        ((D, 896), BF),
        ((D, 128), BF),
        ((896, D), BF),
        ((2 * D, 128), BF),
        ((3, 128, 896), BF),
        ((3, 56, 896), BF),
        ((4, 896, 256), BF),
        ((4, 64, 768), BF),
        ((4, 64, 768), BF),
        ((32, 896), BF),
        ((4, 128, 768), BF),
        ((4, 128, 768), BF),
        ((4, 2, 128, 128), BF),
        ((4, 2, 8, 128), F32),
        ((2, 256, 768), F32),
        ((512, 1024), BF),
        ((2, 4, 256, 256), BF),
        ((2, 4, 128, 256), BF),
        ((2, 3, 128, 256), BF),
        ((2, 2, 128, 128), BF),
        ((2, 4, 128, 128), BF),
        ((2, D, SEQ), BF),
        ((D, SEQ), BF),
        ((2, D, SEQ), BF),
        ((SEQ, D), BF),
        ((SEQ, 896), BF),
        ((SEQ, 896), F32),
        ((D, SEQ), F32),
        ((128, 128), F32),
        ((3, 3, Q, SEQ), BF),
        ((3, 3, Q, SEQ), BF),
        ((3, Q, SEQ), BF),
    ]
    out = pl.pallas_call(
        kernel,
        out_shape=jax.ShapeDtypeStruct((2, Q, SEQ), BF),
        in_specs=[
            hbm, hbm, hbm, hbm, hbm, vmem, hbm, vmem, vmem, smem, hbm, vmem, hbm, hbm, smem,
        ],
        out_specs=hbm,
        scratch_shapes=[pltpu.VMEM(shape, dtype) for shape, dtype in scratch]
        + [
            pltpu.SemaphoreType.DMA((SENDS,)),
            pltpu.SemaphoreType.DMA((SENDS,)),
            pltpu.SemaphoreType.DMA((12,)),
        ],
        compiler_params=pltpu.CompilerParams(
            collective_id=0, has_side_effects=True, vmem_limit_bytes=58 * 1024 * 1024
        ),
    )(
        flip(entering_hidden), flip(entering_embed), flip(incoming_embed), mixer_input_weight[0],
        input_output_matrix_weight[0], flip(step_size_weight), mixer_output_weight[0],
        log_decay_rate, step_size_bias, skip_weight,
        jnp.swapaxes(shared_query_key_value, 0, 1), shared_output_weight, adapter_down[0],
        jnp.swapaxes(adapter_upward[0], 0, 1), calls,
    )
    return jnp.swapaxes(out, 1, 2)[:, None]


def solution(mesh):
    in_specs = (
        P("section", None, "head"),
        P("section", None, "head"),
        P(None, None, "head"),
        P("section", None, "head"),
        P("section", None, None),
        P("section", None, "head"),
        P("section", "head", None),
        P("section", "head"),
        P("section", "head"),
        P("section", "head"),
        P("section", None, "head"),
        P("section", "head"),
        P("section", None, None),
        P("section", None, None, "head"),
        P("section"),
    )
    out_specs = P(None, "section", None, "head")
    return jax.shard_map(
        on_device, mesh=mesh, in_specs=in_specs, out_specs=out_specs, check_vma=False
    )
```

time: 979 us -> 178 us (0.18)
  waiting for transfers between devices: 775 us -> 0 us
  Pallas kernels: 0 us -> 175 us
  matrix products: 70.1 us -> 0 us
  local copies, waits for them, and re-layouts: 60.1 us -> 1.64 us
  blocking collectives: 38.8 us -> 0 us
  between operations: 14.4 us -> 0.66 us
  other arithmetic: 11 us -> 0 us
    all_gather x2 -> x0, waiting for transfers between devices: 572 us -> none  [the longest x1 336 us: on_device(): lax.all_gather(shared_query_key_value, 'section', axis=0, tiled=True)]
    pallas_call x0 -> x1, Pallas kernels: none -> 175 us  [on_device(): pl.pallas_call(kernel, out_shape=jax.ShapeDtypeStruct((2, Q, SEQ), BF), i...]
    psum x2 -> x0, waiting for transfers between devices: 134 us -> none  [on_device(): attn = lax.psum(attn, 'head')]
    unnamed x8 -> x0, waiting for transfers between devices: 67.9 us -> none
    dot_general x20 -> x0, matrix products: 65.5 us -> none  [the longest x2 28.3 us: on_device(): jnp.dot(gate_values, flat_qkv, preferred_element_type=jnp.float32)]
    all_gather x4 -> x0, blocking collectives: 38.8 us -> none  [the longest x2 21.2 us: on_device(): lax.all_gather(embed_rows, 'head', axis=1, tiled=True)]
    all_gather x4 -> x0, local copies, waits for them, and re-layouts: 31.6 us -> none  [the longest x1 25.6 us: on_device(): lax.all_gather(shared_query_key_value, 'section', axis=0, tiled=True)]
    unnamed x30 -> x1, local copies, waits for them, and re-layouts: 13.8 us -> 1.64 us
  transfers between devices with their start and end apart: 8 -> 0, of which waited for: 7 -> 0; matrix products, arithmetic and copies ran while one was open for 2% -> 0% of each run, Pallas kernels for 0% -> 0%
where the time goes in v1:
time: 178 us; the launch traced here: 177 us
  Pallas kernels  175 us (98%)
    pallas_call x1, Pallas kernels, on_device(): pl.pallas_call(kernel, out_shape=jax.ShapeDtypeStruct((2, Q, SEQ), BF), i...  175 us

profile of v1, /device:TPU:1, one launch (start us, length us, event | category | flops | bytes accessed | tf_op | source)
XLA Modules:
  0.0 176.9 jit_solution(1761174534698545547)
XLA Ops:
  0.7 174.6 %shard_map.145 = bf16[2,448,128]{2,1,0:T(8,128)(2,1)} custom-call(bf16[448,128]{1,0:T(8,128)(2,1)} %bitcast.32, bf16[448,128]{1,0:T(8,128)(2,1)} %bitcast.33, bf16[448,128]{1,0:T(8,128)(2,1)} %bitcast.34, bf16[1792,896]{1,0:T(8,128)(2,1)} %bitcast.25, bf16[1792,128]{1,0:T(8,128)(2,1)} %bitcast.30, bf16[14,1792]{1,0:T(8,128)(2,1)} %bitcast.35, ...), custom_call_target="tpu_custom_call" | custom-call | tf_op jit(solution)/shard_map/pallas_call | solution.py:583
  175.2 1.6 copy.19

commit v2 on v1

v2 whole, which is shorter than its diff:
```python
import jax
import jax.numpy as jnp
from jax import lax
from jax.experimental import pallas as pl
from jax.experimental.pallas import tpu as pltpu
from jax.sharding import PartitionSpec as P

MESH = pl.DeviceIdType.MESH
BF = jnp.bfloat16
F32 = jnp.float32
NT = (((1,), (1,)), ((), ()))
TN = (((0,), (0,)), ((), ()))
HIGH = lax.Precision.HIGHEST
D = 1792
Q = 448
SEQ = 128
HEADS = 14
HEAD_WIDTH = 224
EPS = 1e-05
SENDS = 160
POOL = 48


def iota(shape, dim):
    return lax.broadcasted_iota(jnp.int32, shape, dim)


def dot(a, b, dims=(((1,), (0,)), ((), ()))):
    return lax.dot_general(a, b, dims, preferred_element_type=F32)


def silu(v):
    return v / (1.0 + jnp.exp(-v))


def softplus(v):
    return jnp.maximum(v, 0.0) + jnp.log(1.0 + jnp.exp(-jnp.abs(v)))


def kernel(
    h0_in, e0_in, inc_in, wmix_in, wio_in, wdt_ref, wom_in, decay_ref, bias_ref, skip_ref,
    qkv_in, wo_ref, down_in, up_in, calls_ref,
    out_ref,
    xall, xs, wg, wr, rep, lane, wmix, wio, wom, down, up, qw, sel, a2s, a2r, ups, upr, upf, low, misc,
    acc, wog, wo32, mx, rs2s, rs2p, rs2m, atb, atr, mid, hf, mbuf, ubuf, ybuf, xbuf, pbuf, cbuf, rss,
    rsp, rsm,
    outq, send_sem, recv_sem, load_sem,
):
    s = lax.axis_index("section")
    h = lax.axis_index("head")
    x = lax.rem(s, 4)
    y = lax.rem(s // 4, 2)
    z = s // 8
    core = lax.rem(h, 2)
    base = s - x
    sec_up = lax.rem(z + 1, 8) * 8 + lax.rem(s, 8)
    sec_down = lax.rem(z + 7, 8) * 8 + lax.rem(s, 8)
    sec_y = s + 4 - 8 * y
    sec_next = lax.rem(s + 1, 64)
    sec_prev = lax.rem(s + 63, 64)
    x_next = lax.rem(x + 1, 4)
    x_prev = lax.rem(x + 3, 4)
    x_far = lax.rem(x + 2, 4)
    twin = h + 1 - 2 * core
    mate = lax.rem(h + 2, 4)
    far = lax.rem(twin + 2, 4)

    def line(j):
        return lax.rem(x + j, 4)

    index = {}
    descs = {}
    sends = {}

    def only(cond, act):
        if cond is None:
            act()
        else:
            pl.when(cond)(lambda: act())

    pool = {}

    def remote(key, src, dst, section, head):
        at = index.setdefault(key, len(index))
        slot = at % POOL
        before = pool.get(slot)
        if before != key:
            if before is not None:
                only(sends[before], descs[before].wait_send)
            pool[slot] = key
        return pltpu.make_async_remote_copy(
            src_ref=src, dst_ref=dst, send_sem=send_sem.at[slot], recv_sem=recv_sem.at[at],
            device_id={"section": section, "head": head}, device_id_type=MESH,
        )

    def start(key, src, dst, section=None, head=None, cond=None):
        descs[key] = remote(key, src, dst, s if section is None else section, h if head is None else head)
        sends[key] = cond
        only(cond, descs[key].start)

    def pass_on(name, src, dst):
        for key, head in (((name, "same"), h), ((name, "mate"), mate)):
            fresh = remote(key, inc_in, dst, sec_next, head)
            descs[key] = remote(key, src, dst, sec_next, head)
            sends[key] = None
            pl.when(s == 63)(fresh.start)
            pl.when(s != 63)(descs[key].start)

    def pass_got(name, buf_at):
        got(name, "same")
        got(name, "mate")
        for key, rows in (((name, "own"), own), ((name, "other"), rows_of(mate))):
            ref = buf_at(rows)
            start(key, ref, ref, None, twin)

    def pass_wait(name):
        got(name, "own")
        got(name, "other")

    def got(*key, cond=None):
        only(cond, descs[key].wait_recv)

    loads = {}

    def load(name, src, dst):
        loads[name] = pltpu.make_async_copy(src, dst, load_sem.at[len(loads)])
        loads[name].start()

    def rows_of(head):
        return pl.ds(pl.multiple_of(head * Q, Q), Q)

    own = rows_of(h)
    load("qkv", qkv_in, qw)
    load("h0", h0_in, xall.at[x, 0, own])
    load("e0", e0_in, xall.at[x, 1, own])
    load("down", down_in, down)
    load("up", up_in, up)
    load("wmix", wmix_in, wmix)
    load("wio", wio_in, wio)
    load("wom", wom_in, wom)

    barrier = pltpu.get_barrier_semaphore()
    peers = [(base + line(j), h) for j in (1, 2, 3)] + [(s, twin), (s, mate)]
    peers += [(sec_up, h), (sec_down, h), (sec_y, h), (sec_next, h), (sec_prev, h)]
    peers += [(sec_next, mate), (sec_prev, mate)]
    for section, head in peers:
        pl.semaphore_signal(
            barrier, inc=1, device_id={"section": section, "head": head}, device_id_type=MESH
        )
    for i in range(4):
        r, c = iota((896, 256), 0), iota((896, 256), 1)
        sel[i] = jnp.where((r == c + 224 * i) & (c < 224), 1.0, 0.0).astype(BF)
    wo32[...] = jnp.zeros_like(wo32)
    wo32[0:28, :] = wo_ref[...]
    k, c = iota((224, 64), 0), iota((224, 64), 1)
    rep[...] = jnp.where(((k - c) == 56 * ((k >= 56) * 1 + (k >= 112) * 1 + (k >= 168) * 1)) & (c < 56), 1.0, 0.0).astype(BF)
    k, c = iota((224, 128), 0), iota((224, 128), 1)
    lane[...] = jnp.where((c >> 5) == (k >= 56) * 1 + (k >= 112) * 1 + (k >= 168) * 1, 1.0, 0.0).astype(BF)

    def tiles(query, keys, values):
        at = iota((query.shape[0], 128), 1)
        rest = values[:, 128:256]
        return [
            query[:, 0:128],
            keys[:, 0:128],
            values[:, 0:128],
            jnp.where(at < 96, query[:, 128:256], pltpu.roll(rest, 96, axis=1)),
            jnp.where(at < 96, keys[:, 128:256], pltpu.roll(rest, 64, axis=1)),
            jnp.where((at >= 64) & (at < 96), rest, 0.0),
        ]

    loads["qkv"].wait()
    for i in range(4):
        cut = tiles(*[dot(qw[k], sel[i]) for k in range(3)])
        turned = [pltpu.roll(cut[5], shift, axis=1) for shift in (64, 96, 32)]
        cut[5] = jnp.where(
            x == 0, turned[0], jnp.where(x == 1, turned[1], jnp.where(x == 2, cut[5], turned[2]))
        )
        for t in range(6):
            block = jnp.concatenate([cut[t], jnp.zeros((8, 128), F32)], axis=0)
            a2s[i, :, 128 * t : 128 * t + 128] = block.astype(BF)
    pl.semaphore_wait(barrier, len(peers))

    def heads_start(name, src, dst, cond=None):
        start((name, "mate"), src, dst, None, mate, cond)
        start((name, "twin"), src, dst, None, twin, cond)

    def heads_pass(name, buf_at, cond=None):
        got(name, "mate", cond=cond)
        ref = buf_at(rows_of(mate))
        start((name, "pass"), ref, ref, None, twin, cond)

    def heads_wait(name, cond=None):
        got(name, "twin", cond=cond)
        got(name, "pass", cond=cond)

    for j in (1, 2, 3):
        start(("a2a", j), a2s.at[line(j)], a2r.at[x], base + line(j))
    heads_start("h0", h0_in, xall.at[x, 0, own])
    heads_start("e0", e0_in, xall.at[x, 1, own])
    first = x == 0
    fresh = remote(("e1p",), inc_in, xall.at[0, 3, own], sec_next, h)
    descs[("e1p",)] = remote(("e1p",), e0_in, xall.at[0, 3, own], sec_next, h)
    sends[("e1p",)] = x == 3
    pl.when(s == 63)(fresh.start)
    pl.when((x == 3) & (s != 63))(descs[("e1p",)].start)
    a2r[x] = a2s[x]
    r, c = iota((224, 256), 0), iota((224, 256), 1)
    compact = jnp.where(((c - 8 * (c >> 6)) == r) & ((c & 63) < 56), 1.0, 0.0).astype(BF)
    for j in (1, 2, 3):
        got("a2a", j)
    packed = jnp.concatenate([a2r[c, :, 0:640] for c in range(4)], axis=0)
    wg[z, y, 0:224, :] = dot(compact, packed).astype(BF)
    rest = (a2r[0, :, 640:768] + a2r[1, :, 640:768]) + (a2r[2, :, 640:768] + a2r[3, :, 640:768])
    for g in range(4):
        wg[z, y, 224:240, 128 * g : 128 * g + 128] = rest[16 * g : 16 * g + 16]
    wg[z, y, 224:240, 512:640] = jnp.zeros((16, 128), BF)
    wg[z, y, 240:272, :] = wo32[:, 0:640]
    wg[z, y, 272:288, 0:256] = wo32[0:16, 640:896]
    wg[z, y, 272:288, 256:512] = wo32[16:32, 640:896]
    wg[z, y, 272:288, 512:640] = jnp.zeros((16, 128), BF)

    spans = {"all": (0, 288), "w": (0, 240), "w0": (0, 128), "w1": (128, 112), "o": (240, 48)}

    def push(way, other, dz, span="all"):
        first_row, rows = spans[span]
        zz, yy = lax.rem(z + dz + 8, 8), (1 - y) if other else y
        ref = wg.at[zz, yy, pl.ds(first_row, rows)]
        section = {"down": sec_down, "up": sec_up, "y": sec_y}[way]
        start((way, other, dz, span), ref, ref, section)

    def here(way, other, dz, span="all"):
        got(way, other, dz, span)

    def pump(step):
        if step == 0:
            push("down", 0, 0)
            push("up", 0, 0)
            push("y", 0, 0)
        if step == 1:
            here("down", 0, 0)
            push("down", 0, 1)
            push("y", 0, 1)
            here("up", 0, 0)
            push("up", 0, -1)
        if step == 2:
            here("down", 0, 1)
            push("down", 0, 2)
            push("y", 0, 2, "w0")
            here("up", 0, -1)
            push("up", 0, -2)
            push("y", 0, -2, "w1")
            push("y", 0, 2, "w1")
            push("y", 0, -2, "w0")
            push("y", 0, -1, "w")
            for dz in (2, -2, -1):
                push("y", 0, dz, "o")
        if step == 3:
            here("down", 0, 2)
            push("down", 0, 3, "w0")
            here("up", 0, -2)
            push("up", 0, -3, "w1")
        if step == 4:
            here("y", 0, 0)
            here("y", 0, 1)
            here("y", 0, 2, "w0")
            push("down", 1, 2, "w0")
        if step == 5:
            here("y", 0, -2, "w1")
            push("up", 1, -2, "w1")
        if step == 6:
            here("y", 0, 2, "w1")
            push("down", 1, 2, "w1")
        if step == 7:
            here("y", 0, -2, "w0")
            push("up", 1, -2, "w0")
        if step == 8:
            here("down", 1, 2, "w0")
            push("down", 1, 3, "w0")
            here("up", 1, -2, "w1")
            push("up", 1, -3, "w1")
            push("down", 0, 3, "o")
        if step == 9:
            here("y", 0, 2, "o")
            push("down", 1, 2, "o")
            here("y", 0, -2, "o")
            push("up", 1, -2, "o")
        if step == 10:
            here("down", 1, 2, "o")
            push("down", 1, 3, "o")
        if step == 11:
            here("y", 0, -1, "o")
            here("down", 0, 3, "o")
            here("up", 1, -2, "o")
            here("down", 1, 3, "o")

    def unpack(t, carry):
        zz = t // 2
        yy = t - 2 * zz
        at = pl.multiple_of(t * 32, 32)
        wog[pl.ds(at, 32), 0:640] = wg[zz, yy, 240:272, :]
        wog[pl.ds(at, 16), 640:896] = wg[zz, yy, 272:288, 0:256]
        wog[pl.ds(at + 16, 16), 640:896] = wg[zz, yy, 272:288, 256:512]
        return carry

    def line_rows(first, count):
        return pl.ds(pl.multiple_of(core * 896 + first, Q), count)

    def line_start(n):
        ref = xall.at[x, n, line_rows(0, 896)]
        start(("line", n, "next"), ref, ref, base + x_next)
        start(("line", n, "prev"), ref, ref, base + x_prev)

    def line_pass(n):
        got("line", n, "next")
        ref = xall.at[x_prev, n, line_rows(0, 448)]
        start(("line2", n, "next"), ref, ref, base + x_next)
        got("line", n, "prev")
        ref = xall.at[x_next, n, line_rows(448, 448)]
        start(("line2", n, "prev"), ref, ref, base + x_prev)
        for at, key in ((x_prev, 1), (x_next, 2)):
            ref = xall.at[at, n, line_rows(0, 896)]
            start(("share", n, key), ref, ref, None, twin)

    def line_share(n):
        got("line2", n, "next")
        got("line2", n, "prev")
        ref = xall.at[x_far, n, line_rows(0, 896)]
        start(("share", n, 3), ref, ref, None, twin)

    def line_first():
        whole = xall.at[0, 3, line_rows(0, 896)]
        start(("le", "next"), whole, whole, base + 1, None, first)
        start(("le", "prev"), whole, whole, base + 3, None, first)

    def line_first_pass():
        whole = xall.at[0, 3, line_rows(0, 896)]
        for key, at, rows in (("next", 1, line_rows(0, 448)), ("prev", 3, line_rows(448, 448))):
            got("le", key, cond=x == at)
            part = xall.at[0, 3, rows]
            start(("le2", key), part, part, base + 2, None, x == at)
        start(("le", "side"), whole, whole, None, twin, (x == 1) | (x == 3))

    def line_first_share():
        whole = xall.at[0, 3, line_rows(0, 896)]
        for key in ("next", "prev"):
            got("le2", key, cond=x == 2)
        start(("le", "far"), whole, whole, None, twin, x == 2)

    def line_first_wait():
        got("le", "side", cond=(x == 1) | (x == 3))
        got("le", "far", cond=x == 2)

    def line_wait(n):
        for key in (1, 2, 3):
            got("share", n, key)

    def state(c, n):
        if n != 3:
            return c, n
        if isinstance(c, int):
            return (c - 1, 1) if c else (0, 3)
        return jnp.maximum(c - 1, 0), jnp.where(c == 0, 3, 1)

    def row_scale(n):
        total = jnp.zeros((1, SEQ), F32)
        for part in (0, 1):
            def add(t, total):
                block = xall[*state(x, 2 * n + part), pl.ds(pl.multiple_of(t * 128, 128), 128), :].astype(F32)
                return total + jnp.sum(block * block, axis=0, keepdims=True)
            total = lax.fori_loop(0, 14, add, total)
        return lax.rsqrt(total / (2 * D) + EPS)

    def make_low(n):
        scale = row_scale(n)
        total = jnp.zeros((128, SEQ), F32)
        for part in (0, 1):
            total = total + dot(down[part * D : part * D + D, :], xall[*state(x, 2 * n + part)], TN)
        low[x, n] = (total * scale).astype(BF)
        rows = iota((8, 128), 0)
        mark = calls_ref[0].astype(F32)
        misc[x, n] = jnp.where(rows == 0, scale, mark)
        for j in (1, 2, 3):
            start(("low", n, j), low.at[x, n], low.at[x, n], base + line(j))
            start(("misc", n, j), misc.at[x, n], misc.at[x, n], base + line(j))

    def pack_up():
        for i in range(4):
            cut = tiles(*[dot(up[k], sel[i]) for k in range(3)])
            for t in range(6):
                ups[i, :, 128 * t : 128 * t + 128] = cut[t].astype(BF)
        start(("up", "hop"), ups.at[x_far, 64:128], upf, base + x_prev)
        start(("up", "next"), ups.at[x_next], upr.at[x], base + x_next)
        start(("up", "prev"), ups.at[x_prev], upr.at[x], base + x_prev)
        start(("up", "far"), ups.at[x_far, 0:64], upr.at[x, 0:64], base + x_far)
        upr[x] = ups[x]

    def up_pass():
        got("up", "hop")
        start(("up", "last"), upf, upr.at[x_next, 64:128], base + x_prev)

    def up_wait():
        for key in ("next", "prev", "far", "last"):
            got("up", key)

    def wait_low(n):
        for j in (1, 2, 3):
            got("low", n, j)
            got("misc", n, j)

    def eye_column(row, size):
        r, c = iota((size, size), 0), iota((size, size), 1)
        return jnp.sum(jnp.where(r == c, row, 0.0), axis=1, keepdims=True)

    def mixer_in(n, src):
        def add(t, total):
            block = src[pl.ds(pl.multiple_of(t * 128, 128), 128), :].astype(F32)
            return total + jnp.sum(block * block, axis=0, keepdims=True)
        total = lax.fori_loop(0, 14, add, jnp.zeros((1, SEQ), F32))
        scale = lax.rsqrt(total / D + EPS)
        for t in range(14):
            block = src[128 * t : 128 * t + 128, :].astype(F32) * scale
            ubuf[:, 128 * t : 128 * t + 128] = block.T.astype(BF)

        def columns(t, carry):
            at = pl.ds(pl.multiple_of(t * 256, 256), 256)
            xbuf[:, at] = silu(dot(ubuf[...], wmix[:, at]))
            return carry
        lax.fori_loop(0, 3, columns, 0)
        xbuf[:, 768:896] = silu(dot(ubuf[...], wmix[:, 768:896]))

    def mixer_out(n, between=None):
        bc = silu(dot(ubuf[...], wio[...]))
        bias = eye_column(bias_ref[...], HEADS)
        rate = jnp.exp(eye_column(decay_ref[...], HEADS))
        dt = softplus(dot(wdt_ref[...], ubuf[...], NT) + bias)
        upper = jnp.where(iota((128, 128), 0) <= iota((128, 128), 1), 1.0, 0.0)
        cum = lax.dot_general(
            dt * rate, upper, (((1,), (0,)), ((), ())), precision=HIGH, preferred_element_type=F32
        )
        cbuf[...] = jnp.zeros_like(cbuf)
        cbuf[0:HEADS, :] = cum
        cum_t = cbuf[...].T
        lanes = iota((128, 128), 1)
        rolled = pltpu.roll(bc, 64, axis=1)
        inner = lax.dot_general(
            jnp.where(lanes < 64, rolled, 0.0), jnp.where(lanes < 64, bc, 0.0), NT,
            precision=HIGH, preferred_element_type=F32,
        )
        causal = iota((128, 128), 0) >= lanes
        for pair in range(HEADS // 2):
            mixes = []
            for j in (2 * pair, 2 * pair + 1):
                gap = jnp.where(causal, cum[j : j + 1, :] - cum_t[:, j : j + 1], -1e30)
                mixes.append((inner * jnp.exp(gap) * dt[j : j + 1, :]).astype(BF))
            block = xbuf[:, 128 * pair : 128 * pair + 128]
            both = dot(jnp.concatenate(mixes, axis=0), block.astype(BF))
            skip = jnp.where(lanes < 64, skip_ref[0, 2 * pair], skip_ref[0, 2 * pair + 1])
            mixed = jnp.where(lanes < 64, both[0:128], both[128:256]) + skip * block
            ybuf[:, 128 * pair : 128 * pair + 128] = mixed.astype(BF)
        if between is not None:
            between()

        def columns(t, carry):
            at = pl.ds(pl.multiple_of(t * 256, 256), 256)
            part = dot(ybuf[...], wom[:, at])
            pbuf[pl.ds(pl.multiple_of(t * 256, 256), 128), :] = part[:, 0:128].T
            pbuf[pl.ds(pl.multiple_of(t * 256 + 128, 128), 128), :] = part[:, 128:256].T
            return carry
        lax.fori_loop(0, 7, columns, 0)
        rss[n, 0] = pbuf[rows_of(twin), :].astype(BF)
        rss[n, 1] = pbuf[rows_of(far), :].astype(BF)
        start(("rs", n, "twin"), rss.at[n], rsp.at[n], None, twin)

    def mixer_pass(n):
        got("rs", n, "twin")
        rsm[n, 0] = (pbuf[rows_of(mate), :] + rsp[n, 1].astype(F32)).astype(BF)
        start(("rs", n, "mate"), rsm.at[n, 0], rsm.at[n, 1], None, mate)

    def mixer_sum(n, src):
        total = src[own, :].astype(F32) + pbuf[own, :] + rsp[n, 0].astype(F32)
        got("rs", n, "mate")
        outq[n] = (total + rsm[n, 1].astype(F32)).astype(BF)

    def marks():
        return [misc[c, 0, 1:2, :] for c in range(3)]

    def marks_bf():
        return [m.astype(BF) for m in marks()]

    identity = jnp.where(iota((128, 128), 0) == iota((128, 128), 1), 1.0, 0.0).astype(BF)

    def pick(values, masks):
        return values[0] * masks[0] + values[1] * masks[1] + values[2] * masks[2]

    def spread(n, parts=(0, 1)):
        for part in parts:
            places = [state(c, 2 * n + part) for c in range(4)]

            def body(t, carry, part=part, places=places):
                at = pl.ds(pl.multiple_of(t * 224, 224), 224)
                chosen = pick([xall[*places[c], at, :] for c in range(3)], marks_bf())
                xs[n, 8 * part + t, 0:128, :] = dot(identity, chosen, NT).astype(BF)
                xs[n, 8 * part + t, 128:256, :] = dot(identity, xall[*places[3], at, :], NT).astype(BF)
                return carry
            lax.fori_loop(0, 8, body, 0)

    def project(n, other, dz):
        zz, yy = lax.rem(z + dz + 8, 8), (1 - y) if other else y
        rest = jnp.concatenate([wg[zz, yy, 224:240, 128 * g : 128 * g + 128] for g in range(4)], axis=0)
        wr[zz, yy] = (dot(rep[...], rest) * lane[...].astype(F32)).astype(BF)
        project_piece(n, zz, yy)

    def project_piece(n, zz, yy):
        rows = xs[n, 2 * zz + yy]
        acc[n, :, 0:640] += dot(rows, wg[zz, yy, 0:224, :])
        acc[n, :, 640:768] += dot(rows, wr[zz, yy])

    def attend(n):
        up_first = pick([upr[c] for c in range(3)], [m[:, 0:1] for m in marks_bf()])
        low_first = pick([low[c, n] for c in range(3)], marks_bf())
        scale_first = pick([misc[c, n, 0:1, :] for c in range(3)], marks())
        causal = iota((128, 128), 0) >= iota((128, 128), 1)
        for slot in (0, 1):
            low_t = low_first if slot == 0 else low[3, n]
            up_slot = up_first if slot == 0 else upr[3]
            scale = eye_column(scale_first if slot == 0 else misc[3, n, 0:1, :], 128)
            rows = slice(128 * slot, 128 * slot + 128)
            total = acc[n, rows, :] * scale
            rest = total[:, 640:768]
            rest = rest + pltpu.roll(rest, 64, axis=1)
            rest = rest + pltpu.roll(rest, 32, axis=1)
            delta = dot(low_t, up_slot, TN)
            proj = [total[:, 128 * t : 128 * t + 128] + delta[:, 128 * t : 128 * t + 128] for t in range(5)]
            proj.append(rest + delta[:, 640:768])
            at = iota((128, 128), 1)
            tail = jnp.where(
                at < 32,
                pltpu.roll(proj[3], 32, axis=1),
                jnp.where(at < 64, pltpu.roll(proj[4], 64, axis=1), jnp.where(at < 96, proj[5], 0.0)),
            )
            query = jnp.concatenate([proj[0], jnp.where(at < 96, proj[3], 0.0)], axis=1).astype(BF)
            keys = jnp.concatenate([proj[1], jnp.where(at < 96, proj[4], 0.0)], axis=1).astype(BF)
            values = jnp.concatenate([proj[2], tail], axis=1).astype(BF)
            scores = dot(query, keys, NT) * HEAD_WIDTH ** (-0.5)
            scores = jnp.where(causal, scores, -1e30)
            expd = jnp.exp(scores - jnp.max(scores, axis=-1, keepdims=True))
            probs = (expd / jnp.sum(expd, axis=-1, keepdims=True)).astype(BF)
            mixed = dot(probs, values)
            at = pl.multiple_of(224 * x, 32)
            mx[n, pl.ds(at, 128), rows] = mixed[:, 0:128].T.astype(BF)
            mx[n, pl.ds(at + 128, 96), rows] = mixed[:, 128:256].T[0:96].astype(BF)

    def send_mixed(n):
        block = mx.at[n, pl.ds(pl.multiple_of(224 * x, 32), 224)]
        part = mx.at[n, pl.ds(pl.multiple_of(224 * x, 32), 112)]
        start(("mx", n, "prev"), block, block, base + x_prev)
        start(("mx", n, "next"), block, block, base + x_next)
        start(("mx", n, "far"), part, part, base + x_far)

    def pass_mixed(n):
        got("mx", n, "prev")
        part = mx.at[n, pl.ds(pl.multiple_of(224 * x_next + 112, 16), 112)]
        start(("mx", n, "last"), part, part, base + x_prev)

    pt = {}

    def out_project(n):
        for key in ("next", "far", "last"):
            got("mx", n, key)
        for q in range(4):
            rows = slice(128 * q, 128 * q + 128)
            rs2s[n, q] = dot(wog[rows, :], mx[n]).astype(BF)
        start(("rs2", n, 0), rs2s.at[n, twin], rs2p.at[n, 0], None, twin)
        start(("rs2", n, 1), rs2s.at[n, far], rs2p.at[n, 1], None, twin)

    def pass_attn(n):
        got("rs2", n, 1)
        rs2m[n, 0] = (rs2s[n, mate].astype(F32) + rs2p[n, 1].astype(F32)).astype(BF)
        start(("rs2", n, "mate"), rs2m.at[n, 0], rs2m.at[n, 1], None, mate)

    def send_attn(n):
        got("rs2", n, 0)
        got("rs2", n, "mate")
        total = rs2s[n, h].astype(F32) + rs2p[n, 0].astype(F32) + rs2m[n, 1].astype(F32)
        atb[n, 0] = total[:, 0:128].astype(BF)
        atb[n, 1] = total[:, 128:256].astype(BF)
        for j in (1, 2, 3):
            start(("at", n, j), atb.at[n, line(j) // 3], atr.at[n, x], base + line(j))
        atr[n, x] = atb[n, x // 3]

    def make_middle(n):
        for j in (1, 2, 3):
            got("at", n, j)
        r, c = iota((224, 256), 0), iota((224, 256), 1)
        home = (4 * ((c >> 5) & 1) + (c >> 6)) * 28 + (c & 31)
        order = jnp.where((r == home) & ((c & 31) < 28), 1.0, 0.0).astype(BF)
        for half in (0, 1):
            stack = jnp.concatenate([atr[n, i, 64 * half : 64 * half + 64, :] for i in range(4)], axis=0)
            at = pl.ds(pl.multiple_of(h * Q + 224 * half, 224), 224)
            mid[n, at, :] = (xall[x, 2 * n, at, :].astype(F32) + dot(order, stack)).astype(BF)
        heads_start("mid%d" % n, mid.at[n, own], mid.at[n, own])

    def mid_rows(n):
        return lambda rows: mid.at[n, rows]

    mark_here = calls_ref[0].astype(F32)

    def choose(n, plain):
        heads_wait("mid%d" % n)

        def body(t, carry):
            at = pl.ds(pl.multiple_of(t * 128, 128), 128)
            called = mid[n, at, :].astype(F32)
            mbuf[n, at, :] = (called * mark_here + plain[at, :].astype(F32) * (1.0 - mark_here)).astype(BF)
            return carry
        lax.fori_loop(0, 14, body, 0)

    def project_rest(part):
        def body(t, carry):
            zz = t // 2
            project_piece(1, zz, t - 2 * zz)
            return carry
        lax.fori_loop(8 * part, 8 * part + 8, body, 0)

    def state_rows(n):
        return lambda rows: xall.at[x, n, rows]

    pump(0)
    loads["h0"].wait()
    loads["e0"].wait()
    heads_pass("h0", state_rows(0))
    heads_pass("e0", state_rows(1))
    heads_wait("h0")
    line_start(0)
    heads_wait("e0")
    line_start(1)
    got("e1p", cond=first)
    e1_rows = lambda rows: xall.at[0, 3, rows]
    heads_start("e1", e1_rows(own), e1_rows(own), first)
    loads["wmix"].wait()
    mixer_in(0, xall.at[x, 0])
    loads["wio"].wait()
    loads["wom"].wait()
    mixer_out(0)
    pump(1)
    line_pass(0)
    heads_pass("e1", e1_rows, first)
    mixer_pass(0)
    loads["down"].wait()
    make_low(0)
    line_pass(1)
    heads_wait("e1", first)
    line_first()
    line_share(0)
    pump(2)
    mixer_sum(0, xall.at[x, 0])
    pass_on("h1p", outq.at[0], xall.at[x_next, 2, own])
    line_share(1)
    loads["up"].wait()
    pack_up()
    acc[0] = jnp.zeros((256, 768), F32)
    acc[1] = jnp.zeros((256, 768), F32)
    wait_low(0)
    line_wait(0)
    line_wait(1)
    spread(0, (0,))
    pump(3)
    pump(4)
    spread(0, (1,))
    pump(5)
    for dz in (0, 1, -1, 2, -2):
        project(0, 0, dz)
    up_pass()
    pump(6)
    pass_got("h1p", state_rows(2))
    line_first_pass()
    pump(7)
    project(0, 1, 0)
    project(0, 1, 1)
    pump(8)
    pass_wait("h1p")
    line_start(2)
    make_low(1)
    line_first_share()
    here("down", 0, 3, "w0")
    here("up", 0, -3, "w1")
    project(0, 0, 3)
    project(0, 0, -3)
    project(0, 0, 4)
    here("down", 1, 2, "w1")
    here("up", 1, -2, "w0")
    for dz in (2, -2, 3, -3):
        project(0, 1, dz)
    here("y", 0, -1, "w")
    project(0, 1, -1)
    here("down", 1, 3, "w0")
    here("up", 1, -3, "w1")
    project(0, 1, 4)
    up_wait()
    pump(9)
    attend(0)
    send_mixed(0)
    pump(10)
    line_pass(2)
    line_first_wait()
    spread(1, (1,))
    pass_mixed(0)
    project_rest(1)
    pump(11)
    lax.fori_loop(0, 16, unpack, 0)
    line_share(2)
    out_project(0)
    wait_low(1)
    pass_attn(0)
    line_wait(2)
    spread(1, (0,))
    project_rest(0)
    attend(1)
    send_attn(0)
    send_mixed(1)
    make_middle(0)
    pass_mixed(1)
    heads_pass("mid0", mid_rows(0))
    out_project(1)
    choose(0, xall.at[x, 0])
    mixer_in(1, mbuf.at[0])
    pass_attn(1)
    mixer_out(1)
    mixer_pass(1)
    send_attn(1)
    make_middle(1)
    mixer_sum(1, mbuf.at[0])
    pass_on("hfp", outq.at[1], hf.at[own])
    save0 = pltpu.make_async_copy(outq.at[1], out_ref.at[0], load_sem.at[10])
    save0.start()
    heads_pass("mid1", mid_rows(1))
    pass_got("hfp", lambda rows: hf.at[rows])
    pass_wait("hfp")
    choose(1, hf)
    mixer_in(2, mbuf.at[1])
    mixer_out(2)
    mixer_pass(2)
    mixer_sum(2, mbuf.at[1])
    save1 = pltpu.make_async_copy(outq.at[2], out_ref.at[1], load_sem.at[11])
    save1.start()
    assert len(index) <= SENDS, len(index)
    for key in pool.values():
        only(sends[key], descs[key].wait_send)
    save0.wait()
    save1.wait()


def on_device(
    entering_hidden, entering_embed, incoming_embed, mixer_input_weight,
    input_output_matrix_weight, step_size_weight, mixer_output_weight, log_decay_rate,
    step_size_bias, skip_weight, shared_query_key_value, shared_output_weight, adapter_down,
    adapter_upward, calls,
):
    flip = lambda v: jnp.swapaxes(v, 1, 2)[0]
    hbm = pl.BlockSpec(memory_space=pl.ANY)
    vmem = pl.BlockSpec(memory_space=pltpu.VMEM)
    smem = pl.BlockSpec(memory_space=pltpu.SMEM)
    scratch = [
        ((4, 4, D, SEQ), BF),
        ((2, 16, 256, 224), BF),
        ((8, 2, 288, 640), BF),
        ((8, 2, 224, 128), BF),
        ((224, 64), BF),
        ((224, 128), BF),
        ((D, 896), BF),
        ((D, 128), BF),
        ((896, D), BF),
        ((2 * D, 128), BF),
        ((3, 128, 896), BF),
        ((3, 56, 896), BF),
        ((4, 896, 256), BF),
        ((4, 64, 768), BF),
        ((4, 64, 768), BF),
        ((4, 128, 768), BF),
        ((4, 128, 768), BF),
        ((64, 768), BF),
        ((4, 2, 128, 128), BF),
        ((4, 2, 8, 128), F32),
        ((2, 256, 768), F32),
        ((512, 896), BF),
        ((32, 896), BF),
        ((2, 896, 256), BF),
        ((2, 4, 128, 256), BF),
        ((2, 2, 128, 256), BF),
        ((2, 2, 128, 256), BF),
        ((2, 2, 128, 128), BF),
        ((2, 4, 128, 128), BF),
        ((2, D, SEQ), BF),
        ((D, SEQ), BF),
        ((2, D, SEQ), BF),
        ((SEQ, D), BF),
        ((SEQ, 896), BF),
        ((SEQ, 896), F32),
        ((D, SEQ), F32),
        ((128, 128), F32),
        ((3, 2, Q, SEQ), BF),
        ((3, 2, Q, SEQ), BF),
        ((3, 2, Q, SEQ), BF),
        ((3, Q, SEQ), BF),
    ]
    out = pl.pallas_call(
        kernel,
        out_shape=jax.ShapeDtypeStruct((2, Q, SEQ), BF),
        in_specs=[
            hbm, hbm, hbm, hbm, hbm, vmem, hbm, vmem, vmem, smem, hbm, vmem, hbm, hbm, smem,
        ],
        out_specs=hbm,
        scratch_shapes=[pltpu.VMEM(shape, dtype) for shape, dtype in scratch]
        + [
            pltpu.SemaphoreType.DMA((POOL,)),
            pltpu.SemaphoreType.DMA((SENDS,)),
            pltpu.SemaphoreType.DMA((12,)),
        ],
        compiler_params=pltpu.CompilerParams(
            collective_id=0, has_side_effects=True, vmem_limit_bytes=58 * 1024 * 1024
        ),
    )(
        flip(entering_hidden), flip(entering_embed), flip(incoming_embed), mixer_input_weight[0],
        input_output_matrix_weight[0], flip(step_size_weight), mixer_output_weight[0],
        log_decay_rate, step_size_bias, skip_weight,
        jnp.swapaxes(shared_query_key_value, 0, 1), shared_output_weight, adapter_down[0],
        jnp.swapaxes(adapter_upward[0], 0, 1), calls,
    )
    return jnp.swapaxes(out, 1, 2)[:, None]


def solution(mesh):
    in_specs = (
        P("section", None, "head"),
        P("section", None, "head"),
        P(None, None, "head"),
        P("section", None, "head"),
        P("section", None, None),
        P("section", None, "head"),
        P("section", "head", None),
        P("section", "head"),
        P("section", "head"),
        P("section", "head"),
        P("section", None, "head"),
        P("section", "head"),
        P("section", None, None),
        P("section", None, None, "head"),
        P("section"),
    )
    out_specs = P(None, "section", None, "head")
    return jax.shard_map(
        on_device, mesh=mesh, in_specs=in_specs, out_specs=out_specs, check_vma=False
    )
```

time: 178 us -> 131 us (0.74)
  Pallas kernels: 175 us -> 128 us
    pallas_call x1, Pallas kernels: 175 us -> 128 us  [on_device(): pl.pallas_call(kernel, out_shape=jax.ShapeDtypeStruct((2, Q, SEQ), BF), i...]
where the time goes in v2:
time: 131 us; the launch traced here: 130 us
  Pallas kernels  128 us (98%)
  local copies, waits for them, and re-layouts  1.64 us (1%)
    pallas_call x1, Pallas kernels, on_device(): pl.pallas_call(kernel, out_shape=jax.ShapeDtypeStruct((2, Q, SEQ), BF), i...  128 us

profile of v2, /device:TPU:1, one launch (start us, length us, event | category | flops | bytes accessed | tf_op | source)
XLA Modules:
  0.0 130.2 jit_solution(2136380719817733197)
XLA Ops:
  0.7 127.9 %shard_map.145 = bf16[2,448,128]{2,1,0:T(8,128)(2,1)} custom-call(bf16[448,128]{1,0:T(8,128)(2,1)} %bitcast.32, bf16[448,128]{1,0:T(8,128)(2,1)} %bitcast.33, bf16[448,128]{1,0:T(8,128)(2,1)} %bitcast.34, bf16[1792,896]{1,0:T(8,128)(2,1)} %bitcast.25, bf16[1792,128]{1,0:T(8,128)(2,1)} %bitcast.30, bf16[14,1792]{1,0:T(8,128)(2,1)} %bitcast.35, ...), custom_call_target="tpu_custom_call" | custom-call | tf_op jit(solution)/shard_map/pallas_call | solution.py:807
  128.5 1.6 %copy.19 = bf16[2,1,128,448]{2,3,1,0:T(8,128)(2,1)} copy(bf16[2,1,128,448]{2,3,1,0:T(8,128)(2,1)} %bitcast.27) | data formatting | bytes 458752

commit v3 on v2

--- a/solution.py
+++ b/solution.py
@@ -17,7 +17,7 @@
 HEADS = 14
 HEAD_WIDTH = 224
 EPS = 1e-05
-SENDS = 160
+SENDS = 133
 POOL = 48
 
 
@@ -41,8 +41,8 @@
     h0_in, e0_in, inc_in, wmix_in, wio_in, wdt_ref, wom_in, decay_ref, bias_ref, skip_ref,
     qkv_in, wo_ref, down_in, up_in, calls_ref,
     out_ref,
-    xall, xs, wg, wr, rep, lane, wmix, wio, wom, down, up, qw, sel, a2s, a2r, ups, upr, upf, low, misc,
-    acc, wog, wo32, mx, rs2s, rs2p, rs2m, atb, atr, mid, hf, mbuf, ubuf, ybuf, xbuf, pbuf, cbuf, rss,
+    xall, xs, wg, wr, rep, lane, wmix, wom, wom4, down, up, qw, a2s, a2r, ups, upr, low, misc,
+    acc, wog, wo32, mx, rs2s, rs2r, atb, atr, mid, hf, mbuf, ubuf, ybuf, xbuf, pbuf, sbuf, cbuf, rss,
     rsp, rsm,
     outq, send_sem, recv_sem, load_sem,
 ):
@@ -99,7 +99,7 @@
         only(cond, descs[key].start)
 
     def pass_on(name, src, dst):
-        for key, head in (((name, "same"), h), ((name, "mate"), mate)):
+        for key, head in (((name, "mate"), mate), ((name, "same"), h)):
             fresh = remote(key, inc_in, dst, sec_next, head)
             descs[key] = remote(key, src, dst, sec_next, head)
             sends[key] = None
@@ -135,27 +135,34 @@
     load("e0", e0_in, xall.at[x, 1, own])
     load("down", down_in, down)
     load("up", up_in, up)
-    load("wmix", wmix_in, wmix)
-    load("wio", wio_in, wio)
+    load("wmix", wmix_in, wmix.at[:, pl.ds(0, 896)])
+    load("wio", wio_in, wmix.at[:, pl.ds(896, 128)])
     load("wom", wom_in, wom)
 
     barrier = pltpu.get_barrier_semaphore()
-    peers = [(base + line(j), h) for j in (1, 2, 3)] + [(s, twin), (s, mate)]
+    peers = [(base + line(j), h) for j in (1, 2, 3)] + [(s, twin), (s, mate), (s, far)]
     peers += [(sec_up, h), (sec_down, h), (sec_y, h), (sec_next, h), (sec_prev, h)]
     peers += [(sec_next, mate), (sec_prev, mate)]
     for section, head in peers:
         pl.semaphore_signal(
             barrier, inc=1, device_id={"section": section, "head": head}, device_id_type=MESH
         )
-    for i in range(4):
-        r, c = iota((896, 256), 0), iota((896, 256), 1)
-        sel[i] = jnp.where((r == c + 224 * i) & (c < 224), 1.0, 0.0).astype(BF)
+    def head_columns(block, i):
+        first_tile = 224 * i // 128 * 128
+        window = block[:, first_tile : min(first_tile + 384, 896)]
+        width = window.shape[1]
+        shift = (width - (224 * i - first_tile)) % width
+        return (pltpu.roll(window, shift, axis=1) if shift else window)[:, 0:256]
+
     wo32[...] = jnp.zeros_like(wo32)
     wo32[0:28, :] = wo_ref[...]
+    def owner(k):
+        return (k >= 56) * 1 + (k >= 112) * 1 + (k >= 168) * 1
+
     k, c = iota((224, 64), 0), iota((224, 64), 1)
-    rep[...] = jnp.where(((k - c) == 56 * ((k >= 56) * 1 + (k >= 112) * 1 + (k >= 168) * 1)) & (c < 56), 1.0, 0.0).astype(BF)
+    rep[...] = jnp.where(16 * owner(k) + ((k - 56 * owner(k)) & 15) == c, 1.0, 0.0).astype(BF)
     k, c = iota((224, 128), 0), iota((224, 128), 1)
-    lane[...] = jnp.where((c >> 5) == (k >= 56) * 1 + (k >= 112) * 1 + (k >= 168) * 1, 1.0, 0.0).astype(BF)
+    lane[...] = jnp.where((c >> 5) == ((k - 56 * owner(k)) >> 4), 1.0, 0.0).astype(BF)
 
     def tiles(query, keys, values):
         at = iota((query.shape[0], 128), 1)
@@ -170,15 +177,16 @@
         ]
 
     loads["qkv"].wait()
+    blocks = [qw[k].astype(F32) for k in range(3)]
+    nothing = jnp.zeros((8, 128), F32)
     for i in range(4):
-        cut = tiles(*[dot(qw[k], sel[i]) for k in range(3)])
-        turned = [pltpu.roll(cut[5], shift, axis=1) for shift in (64, 96, 32)]
-        cut[5] = jnp.where(
-            x == 0, turned[0], jnp.where(x == 1, turned[1], jnp.where(x == 2, cut[5], turned[2]))
-        )
-        for t in range(6):
-            block = jnp.concatenate([cut[t], jnp.zeros((8, 128), F32)], axis=0)
-            a2s[i, :, 128 * t : 128 * t + 128] = block.astype(BF)
+        cut = tiles(*[head_columns(blocks[k], i) for k in range(3)])
+        last = jnp.concatenate([cut[5][48:56], nothing], axis=0)
+        folded = pltpu.roll(cut[5][0:16], 64, axis=1) + pltpu.roll(cut[5][16:32], 96, axis=1)
+        folded = folded + cut[5][32:48] + pltpu.roll(last, 32, axis=1)
+        for t in range(5):
+            spare = folded[8 * t : 8 * t + 8] if t < 2 else nothing
+            a2s[i, :, 128 * t : 128 * t + 128] = jnp.concatenate([cut[t], spare], axis=0).astype(BF)
     pl.semaphore_wait(barrier, len(peers))
 
     def heads_start(name, src, dst, cond=None):
@@ -194,7 +202,7 @@
         got(name, "twin", cond=cond)
         got(name, "pass", cond=cond)
 
-    for j in (1, 2, 3):
+    for j in (2, 1, 3):
         start(("a2a", j), a2s.at[line(j)], a2r.at[x], base + line(j))
     heads_start("h0", h0_in, xall.at[x, 0, own])
     heads_start("e0", e0_in, xall.at[x, 1, own])
@@ -209,60 +217,72 @@
     compact = jnp.where(((c - 8 * (c >> 6)) == r) & ((c & 63) < 56), 1.0, 0.0).astype(BF)
     for j in (1, 2, 3):
         got("a2a", j)
-    packed = jnp.concatenate([a2r[c, :, 0:640] for c in range(4)], axis=0)
+    packed = jnp.concatenate([a2r[c] for c in range(4)], axis=0)
     wg[z, y, 0:224, :] = dot(compact, packed).astype(BF)
-    rest = (a2r[0, :, 640:768] + a2r[1, :, 640:768]) + (a2r[2, :, 640:768] + a2r[3, :, 640:768])
-    for g in range(4):
-        wg[z, y, 224:240, 128 * g : 128 * g + 128] = rest[16 * g : 16 * g + 16]
+    for c in range(4):
+        rest = [a2r[c, 48:64, 128 * t : 128 * t + 128].astype(F32)[8:16] for t in (0, 1)]
+        wg[z, y, 224:240, 128 * c : 128 * c + 128] = jnp.concatenate(rest, axis=0).astype(BF)
     wg[z, y, 224:240, 512:640] = jnp.zeros((16, 128), BF)
     wg[z, y, 240:272, :] = wo32[:, 0:640]
     wg[z, y, 272:288, 0:256] = wo32[0:16, 640:896]
     wg[z, y, 272:288, 256:512] = wo32[16:32, 640:896]
     wg[z, y, 272:288, 512:640] = jnp.zeros((16, 128), BF)
 
-    spans = {"all": (0, 288), "w": (0, 240), "w0": (0, 128), "w1": (128, 112), "o": (240, 48)}
-
-    def push(way, other, dz, span="all"):
+    spans = {"c0": (0, 128), "c1": (128, 160), "w0": (0, 128), "w1": (128, 112), "o": (240, 48)}
+
+    def push(way, other, dz, span):
         first_row, rows = spans[span]
         zz, yy = lax.rem(z + dz + 8, 8), (1 - y) if other else y
         ref = wg.at[zz, yy, pl.ds(first_row, rows)]
         section = {"down": sec_down, "up": sec_up, "y": sec_y}[way]
         start((way, other, dz, span), ref, ref, section)
 
-    def here(way, other, dz, span="all"):
+    def here(way, other, dz, span):
         got(way, other, dz, span)
 
     def pump(step):
         if step == 0:
-            push("down", 0, 0)
-            push("up", 0, 0)
-            push("y", 0, 0)
-        if step == 1:
-            here("down", 0, 0)
-            push("down", 0, 1)
-            push("y", 0, 1)
-            here("up", 0, 0)
-            push("up", 0, -1)
+            for span in ("c0", "c1"):
+                push("down", 0, 0, span)
+                push("up", 0, 0, span)
+                push("y", 0, 0, span)
+        for at, span in ((1, "c0"), (1.5, "c1")):
+            if step == at:
+                here("down", 0, 0, span)
+                push("down", 0, 1, span)
+                push("y", 0, 1, span)
+                here("up", 0, 0, span)
+                push("up", 0, -1, span)
         if step == 2:
-            here("down", 0, 1)
-            push("down", 0, 2)
+            here("down", 0, 1, "c0")
+            push("down", 0, 2, "c0")
             push("y", 0, 2, "w0")
-            here("up", 0, -1)
-            push("up", 0, -2)
+            here("up", 0, -1, "c0")
+            push("up", 0, -2, "c0")
+        if step == 2.5:
+            here("down", 0, 1, "c1")
+            push("down", 0, 2, "c1")
+            here("up", 0, -1, "c1")
+            push("up", 0, -2, "c1")
             push("y", 0, -2, "w1")
             push("y", 0, 2, "w1")
             push("y", 0, -2, "w0")
-            push("y", 0, -1, "w")
+            push("y", 0, -1, "w1")
             for dz in (2, -2, -1):
                 push("y", 0, dz, "o")
+            here("y", 0, 0, "c0")
+            push("up", 1, 0, "w0")
         if step == 3:
-            here("down", 0, 2)
+            here("down", 0, 2, "c0")
             push("down", 0, 3, "w0")
-            here("up", 0, -2)
+            here("up", 0, -2, "c0")
+            here("up", 0, -2, "c1")
             push("up", 0, -3, "w1")
+            here("down", 0, 2, "c1")
+            here("y", 0, 0, "c1")
         if step == 4:
-            here("y", 0, 0)
-            here("y", 0, 1)
+            here("y", 0, 1, "c0")
+            here("y", 0, 1, "c1")
             here("y", 0, 2, "w0")
             push("down", 1, 2, "w0")
         if step == 5:
@@ -294,14 +314,13 @@
             here("up", 1, -2, "o")
             here("down", 1, 3, "o")
 
-    def unpack(t, carry):
-        zz = t // 2
-        yy = t - 2 * zz
-        at = pl.multiple_of(t * 32, 32)
-        wog[pl.ds(at, 32), 0:640] = wg[zz, yy, 240:272, :]
-        wog[pl.ds(at, 16), 640:896] = wg[zz, yy, 272:288, 0:256]
-        wog[pl.ds(at + 16, 16), 640:896] = wg[zz, yy, 272:288, 256:512]
-        return carry
+    def unpack(other, places):
+        for dz in places:
+            zz, yy = lax.rem(z + dz + 8, 8), (1 - y) if other else y
+            at = pl.multiple_of(zz * 64 + yy * 32, 32)
+            wog[pl.ds(at, 32), 0:640] = wg[zz, yy, 240:272, :]
+            wog[pl.ds(at, 16), 640:896] = wg[zz, yy, 272:288, 0:256]
+            wog[pl.ds(at + 16, 16), 640:896] = wg[zz, yy, 272:288, 256:512]
 
     def line_rows(first, count):
         return pl.ds(pl.multiple_of(core * 896 + first, Q), count)
@@ -385,22 +404,18 @@
             start(("misc", n, j), misc.at[x, n], misc.at[x, n], base + line(j))
 
     def pack_up():
+        blocks = [up[k].astype(F32) for k in range(3)]
         for i in range(4):
-            cut = tiles(*[dot(up[k], sel[i]) for k in range(3)])
+            cut = tiles(*[head_columns(blocks[k], i) for k in range(3)])
             for t in range(6):
                 ups[i, :, 128 * t : 128 * t + 128] = cut[t].astype(BF)
-        start(("up", "hop"), ups.at[x_far, 64:128], upf, base + x_prev)
+        start(("up", "far"), ups.at[x_far], upr.at[x], base + x_far)
         start(("up", "next"), ups.at[x_next], upr.at[x], base + x_next)
         start(("up", "prev"), ups.at[x_prev], upr.at[x], base + x_prev)
-        start(("up", "far"), ups.at[x_far, 0:64], upr.at[x, 0:64], base + x_far)
         upr[x] = ups[x]
 
-    def up_pass():
-        got("up", "hop")
-        start(("up", "last"), upf, upr.at[x_next, 64:128], base + x_prev)
-
     def up_wait():
-        for key in ("next", "prev", "far", "last"):
+        for key in ("next", "prev", "far"):
             got("up", key)
 
     def wait_low(n):
@@ -412,28 +427,55 @@
         r, c = iota((size, size), 0), iota((size, size), 1)
         return jnp.sum(jnp.where(r == c, row, 0.0), axis=1, keepdims=True)
 
-    def mixer_in(n, src):
-        def add(t, total):
-            block = src[pl.ds(pl.multiple_of(t * 128, 128), 128), :].astype(F32)
-            return total + jnp.sum(block * block, axis=0, keepdims=True)
-        total = lax.fori_loop(0, 14, add, jnp.zeros((1, SEQ), F32))
-        scale = lax.rsqrt(total / D + EPS)
+    def mixer_weights():
+        cbuf[...] = jnp.zeros_like(cbuf)
         for t in range(14):
-            block = src[128 * t : 128 * t + 128, :].astype(F32) * scale
-            ubuf[:, 128 * t : 128 * t + 128] = block.T.astype(BF)
-
-        def columns(t, carry):
-            at = pl.ds(pl.multiple_of(t * 256, 256), 256)
-            xbuf[:, at] = silu(dot(ubuf[...], wmix[:, at]))
+            cbuf[0:HEADS, :] = wdt_ref[:, 128 * t : 128 * t + 128].astype(F32)
+            wmix[128 * t : 128 * t + 128, 1024:1152] = cbuf[...].T.astype(BF)
+            wmix[128 * t : 128 * t + 128, 1152:1280] = jnp.zeros((128, 128), BF)
+
+    def mixer_quarters():
+        def body(t, carry):
+            rows = pl.ds(pl.multiple_of(t * 128, 128), 128)
+            low_lanes = iota((128, 128), 1) < 64
+            for q in (0, 2):
+                wom4[q, rows, 0:448] = wom[rows, 448 * q : 448 * q + 448]
+            for q in (1, 3):
+                first_tile = (448 * q - 64) // 128
+                turned = [
+                    pltpu.roll(wom[rows, 128 * k : 128 * k + 128].astype(F32), 64, axis=1)
+                    for k in range(first_tile, first_tile + 4)
+                ]
+                for k in range(3):
+                    wom4[q, rows, 128 * k : 128 * k + 128] = jnp.where(low_lanes, turned[k], turned[k + 1]).astype(BF)
+                wom4[q, rows, 384:512] = jnp.where(low_lanes, turned[3], 0.0).astype(BF)
+            for q in (0, 2):
+                wom4[q, rows, 448:512] = jnp.zeros((128, 64), BF)
             return carry
-        lax.fori_loop(0, 3, columns, 0)
-        xbuf[:, 768:896] = silu(dot(ubuf[...], wmix[:, 768:896]))
+        lax.fori_loop(0, 7, body, 0)
+
+    def quarter_in(q, block, slot):
+        total = jnp.sum(block * block, axis=0, keepdims=True)
+        for t in range(3):
+            ubuf[:, 128 * t : 128 * t + 128] = block[128 * t : 128 * t + 128].T.astype(BF)
+        rest = jnp.concatenate([block[384:448], jnp.zeros((64, SEQ), F32)], axis=0)
+        ubuf[:, 384:512] = rest.T.astype(BF)
+        rows = rows_of(q)
+
+        for t in range(5):
+            xbuf[slot, :, 256 * t : 256 * t + 256] = dot(ubuf[:, 0:448], wmix[rows, 256 * t : 256 * t + 256])
+        sbuf[slot : slot + 1, :] = total
+
+    def mixed_columns(first_column):
+        at = slice(first_column, first_column + 128)
+        return (xbuf[0, :, at] + xbuf[1, :, at]) + (xbuf[2, :, at] + xbuf[3, :, at])
 
     def mixer_out(n, between=None):
-        bc = silu(dot(ubuf[...], wio[...]))
+        scale = eye_column(lax.rsqrt(jnp.sum(sbuf[0:4, :], axis=0, keepdims=True) / D + EPS), 128)
+        bc = silu(mixed_columns(896) * scale)
         bias = eye_column(bias_ref[...], HEADS)
         rate = jnp.exp(eye_column(decay_ref[...], HEADS))
-        dt = softplus(dot(wdt_ref[...], ubuf[...], NT) + bias)
+        dt = softplus((mixed_columns(1024) * scale).T[0:HEADS] + bias)
         upper = jnp.where(iota((128, 128), 0) <= iota((128, 128), 1), 1.0, 0.0)
         cum = lax.dot_general(
             dt * rate, upper, (((1,), (0,)), ((), ())), precision=HIGH, preferred_element_type=F32
@@ -453,32 +495,38 @@
             for j in (2 * pair, 2 * pair + 1):
                 gap = jnp.where(causal, cum[j : j + 1, :] - cum_t[:, j : j + 1], -1e30)
                 mixes.append((inner * jnp.exp(gap) * dt[j : j + 1, :]).astype(BF))
-            block = xbuf[:, 128 * pair : 128 * pair + 128]
+            block = silu(mixed_columns(128 * pair) * scale)
             both = dot(jnp.concatenate(mixes, axis=0), block.astype(BF))
             skip = jnp.where(lanes < 64, skip_ref[0, 2 * pair], skip_ref[0, 2 * pair + 1])
             mixed = jnp.where(lanes < 64, both[0:128], both[128:256]) + skip * block
             ybuf[:, 128 * pair : 128 * pair + 128] = mixed.astype(BF)
+
+        def quarter(q):
+            def columns(t, carry):
+                at = pl.multiple_of(t * 256, 256)
+                part = dot(ybuf[...], wom4[q, :, pl.ds(at, 256)])
+                pbuf[q, pl.ds(at, 128), :] = part[:, 0:128].T
+                pbuf[q, pl.ds(at + 128, 128), :] = part[:, 128:256].T
+                return carry
+            lax.fori_loop(0, 2, columns, 0)
+
+        quarter(far)
+        rss[n, 1] = pbuf[far, 0:Q, :].astype(BF)
+        start(("rs", n, "far"), rss.at[n, 1], rsp.at[n, 1], None, twin)
+        quarter(mate)
+        got("rs", n, "far")
+        rsm[n, 0] = (pbuf[mate, 0:Q, :] + rsp[n, 1].astype(F32)).astype(BF)
+        start(("rs", n, "mate"), rsm.at[n, 0], rsm.at[n, 1], None, mate)
         if between is not None:
             between()
-
-        def columns(t, carry):
-            at = pl.ds(pl.multiple_of(t * 256, 256), 256)
-            part = dot(ybuf[...], wom[:, at])
-            pbuf[pl.ds(pl.multiple_of(t * 256, 256), 128), :] = part[:, 0:128].T
-            pbuf[pl.ds(pl.multiple_of(t * 256 + 128, 128), 128), :] = part[:, 128:256].T
-            return carry
-        lax.fori_loop(0, 7, columns, 0)
-        rss[n, 0] = pbuf[rows_of(twin), :].astype(BF)
-        rss[n, 1] = pbuf[rows_of(far), :].astype(BF)
-        start(("rs", n, "twin"), rss.at[n], rsp.at[n], None, twin)
-
-    def mixer_pass(n):
+        quarter(twin)
+        rss[n, 0] = pbuf[twin, 0:Q, :].astype(BF)
+        start(("rs", n, "twin"), rss.at[n, 0], rsp.at[n, 0], None, twin)
+        quarter(h)
+
+    def mixer_sum(n, src):
         got("rs", n, "twin")
-        rsm[n, 0] = (pbuf[rows_of(mate), :] + rsp[n, 1].astype(F32)).astype(BF)
-        start(("rs", n, "mate"), rsm.at[n, 0], rsm.at[n, 1], None, mate)
-
-    def mixer_sum(n, src):
-        total = src[own, :].astype(F32) + pbuf[own, :] + rsp[n, 0].astype(F32)
+        total = src[own, :].astype(F32) + pbuf[h, 0:Q, :] + rsp[n, 0].astype(F32)
         got("rs", n, "mate")
         outq[n] = (total + rsm[n, 1].astype(F32)).astype(BF)
 
@@ -553,39 +601,29 @@
 
     def send_mixed(n):
         block = mx.at[n, pl.ds(pl.multiple_of(224 * x, 32), 224)]
-        part = mx.at[n, pl.ds(pl.multiple_of(224 * x, 32), 112)]
+        start(("mx", n, "far"), block, block, base + x_far)
         start(("mx", n, "prev"), block, block, base + x_prev)
         start(("mx", n, "next"), block, block, base + x_next)
-        start(("mx", n, "far"), part, part, base + x_far)
-
-    def pass_mixed(n):
-        got("mx", n, "prev")
-        part = mx.at[n, pl.ds(pl.multiple_of(224 * x_next + 112, 16), 112)]
-        start(("mx", n, "last"), part, part, base + x_prev)
 
     pt = {}
 
     def out_project(n):
-        for key in ("next", "far", "last"):
+        for key in ("prev", "next", "far"):
             got("mx", n, key)
         for q in range(4):
             rows = slice(128 * q, 128 * q + 128)
             rs2s[n, q] = dot(wog[rows, :], mx[n]).astype(BF)
-        start(("rs2", n, 0), rs2s.at[n, twin], rs2p.at[n, 0], None, twin)
-        start(("rs2", n, 1), rs2s.at[n, far], rs2p.at[n, 1], None, twin)
-
-    def pass_attn(n):
-        got("rs2", n, 1)
-        rs2m[n, 0] = (rs2s[n, mate].astype(F32) + rs2p[n, 1].astype(F32)).astype(BF)
-        start(("rs2", n, "mate"), rs2m.at[n, 0], rs2m.at[n, 1], None, mate)
+        for key, head in ((0, far), (1, mate), (2, twin)):
+            start(("rs2", n, key), rs2s.at[n, head], rs2r.at[n, key], None, head)
 
     def send_attn(n):
-        got("rs2", n, 0)
-        got("rs2", n, "mate")
-        total = rs2s[n, h].astype(F32) + rs2p[n, 0].astype(F32) + rs2m[n, 1].astype(F32)
+        total = rs2s[n, h].astype(F32)
+        for key in (2, 1, 0):
+            got("rs2", n, key)
+            total = total + rs2r[n, key].astype(F32)
         atb[n, 0] = total[:, 0:128].astype(BF)
         atb[n, 1] = total[:, 128:256].astype(BF)
-        for j in (1, 2, 3):
+        for j in (2, 1, 3):
             start(("at", n, j), atb.at[n, line(j) // 3], atr.at[n, x], base + line(j))
         atr[n, x] = atb[n, x // 3]
 
@@ -606,22 +644,20 @@
 
     mark_here = calls_ref[0].astype(F32)
 
-    def choose(n, plain):
-        heads_wait("mid%d" % n)
-
-        def body(t, carry):
-            at = pl.ds(pl.multiple_of(t * 128, 128), 128)
-            called = mid[n, at, :].astype(F32)
-            mbuf[n, at, :] = (called * mark_here + plain[at, :].astype(F32) * (1.0 - mark_here)).astype(BF)
-            return carry
-        lax.fori_loop(0, 14, body, 0)
-
-    def project_rest(part):
+    def choose(n, q, plain, slot):
+        rows = rows_of(q)
+        called = mid[n, rows, :].astype(F32)
+        block = (called * mark_here + plain[rows, :].astype(F32) * (1.0 - mark_here)).astype(BF)
+        if slot == 0:
+            mbuf[n, rows, :] = block
+        quarter_in(q, block.astype(F32), slot)
+
+    def project_rest(first_piece, end):
         def body(t, carry):
             zz = t // 2
             project_piece(1, zz, t - 2 * zz)
             return carry
-        lax.fori_loop(8 * part, 8 * part + 8, body, 0)
+        lax.fori_loop(first_piece, end, body, 0)
 
     def state_rows(n):
         return lambda rows: xall.at[x, n, rows]
@@ -639,21 +675,25 @@
     e1_rows = lambda rows: xall.at[0, 3, rows]
     heads_start("e1", e1_rows(own), e1_rows(own), first)
     loads["wmix"].wait()
-    mixer_in(0, xall.at[x, 0])
     loads["wio"].wait()
+    mixer_weights()
+    for q in range(4):
+        quarter_in(q, xall[x, 0, Q * q : Q * q + Q, :].astype(F32), q)
     loads["wom"].wait()
+    mixer_quarters()
+    pump(1)
     mixer_out(0)
-    pump(1)
+    pump(1.5)
     line_pass(0)
     heads_pass("e1", e1_rows, first)
-    mixer_pass(0)
     loads["down"].wait()
     make_low(0)
     line_pass(1)
+    pump(2)
     heads_wait("e1", first)
     line_first()
     line_share(0)
-    pump(2)
+    pump(2.5)
     mixer_sum(0, xall.at[x, 0])
     pass_on("h1p", outq.at[0], xall.at[x_next, 2, own])
     line_share(1)
@@ -667,22 +707,25 @@
     spread(0, (0,))
     pump(3)
     pump(4)
+    line_first_pass()
     spread(0, (1,))
     pump(5)
     for dz in (0, 1, -1, 2, -2):
         project(0, 0, dz)
-    up_pass()
     pump(6)
+    line_first_share()
+    unpack(0, (0, 1, -1, 2, -2, 3, -3))
+    unpack(1, (0, 1))
     pass_got("h1p", state_rows(2))
-    line_first_pass()
+    line_first_wait()
+    spread(1, (1,))
     pump(7)
+    pump(8)
     project(0, 1, 0)
     project(0, 1, 1)
-    pump(8)
     pass_wait("h1p")
     line_start(2)
     make_low(1)
-    line_first_share()
     here("down", 0, 3, "w0")
     here("up", 0, -3, "w1")
     project(0, 0, 3)
@@ -692,7 +735,8 @@
     here("up", 1, -2, "w0")
     for dz in (2, -2, 3, -3):
         project(0, 1, dz)
-    here("y", 0, -1, "w")
+    here("y", 0, -1, "w1")
+    here("up", 1, 0, "w0")
     project(0, 1, -1)
     here("down", 1, 3, "w0")
     here("up", 1, -3, "w1")
@@ -703,32 +747,29 @@
     send_mixed(0)
     pump(10)
     line_pass(2)
-    line_first_wait()
-    spread(1, (1,))
-    pass_mixed(0)
-    project_rest(1)
+    project_rest(8, 16)
     pump(11)
-    lax.fori_loop(0, 16, unpack, 0)
+    unpack(0, (4,))
+    unpack(1, (-1, 2, -2, 3, -3, 4))
+    out_project(0)
     line_share(2)
-    out_project(0)
     wait_low(1)
-    pass_attn(0)
     line_wait(2)
     spread(1, (0,))
-    project_rest(0)
+    send_attn(0)
+    project_rest(0, 8)
     attend(1)
-    send_attn(0)
     send_mixed(1)
     make_middle(0)
-    pass_mixed(1)
+    choose(0, h, xall.at[x, 0], 0)
+    got("mid0", "twin")
+    choose(0, twin, xall.at[x, 0], 1)
     heads_pass("mid0", mid_rows(0))
     out_project(1)
-    choose(0, xall.at[x, 0])
-    mixer_in(1, mbuf.at[0])
-    pass_attn(1)
-    mixer_out(1)
-    mixer_pass(1)
-    send_attn(1)
+    choose(0, mate, xall.at[x, 0], 2)
+    got("mid0", "pass")
+    choose(0, far, xall.at[x, 0], 3)
+    mixer_out(1, lambda: send_attn(1))
     make_middle(1)
     mixer_sum(1, mbuf.at[0])
     pass_on("hfp", outq.at[1], hf.at[own])
@@ -736,15 +777,17 @@
     save0.start()
     heads_pass("mid1", mid_rows(1))
     pass_got("hfp", lambda rows: hf.at[rows])
+    choose(1, h, hf, 0)
+    choose(1, mate, hf, 1)
+    heads_wait("mid1")
     pass_wait("hfp")
-    choose(1, hf)
-    mixer_in(2, mbuf.at[1])
+    choose(1, twin, hf, 2)
+    choose(1, far, hf, 3)
     mixer_out(2)
-    mixer_pass(2)
     mixer_sum(2, mbuf.at[1])
     save1 = pltpu.make_async_copy(outq.at[2], out_ref.at[1], load_sem.at[11])
     save1.start()
-    assert len(index) <= SENDS, len(index)
+    assert len(index) == SENDS, len(index)
     for key in pool.values():
         only(sends[key], descs[key].wait_send)
     save0.wait()
@@ -768,18 +811,16 @@
         ((8, 2, 224, 128), BF),
         ((224, 64), BF),
         ((224, 128), BF),
-        ((D, 896), BF),
-        ((D, 128), BF),
+        ((D, 1280), BF),
         ((896, D), BF),
+        ((4, 896, 512), BF),
         ((2 * D, 128), BF),
         ((3, 128, 896), BF),
         ((3, 56, 896), BF),
-        ((4, 896, 256), BF),
-        ((4, 64, 768), BF),
-        ((4, 64, 768), BF),
+        ((4, 64, 640), BF),
+        ((4, 64, 640), BF),
         ((4, 128, 768), BF),
         ((4, 128, 768), BF),
-        ((64, 768), BF),
         ((4, 2, 128, 128), BF),
         ((4, 2, 8, 128), F32),
         ((2, 256, 768), F32),
@@ -787,17 +828,17 @@
         ((32, 896), BF),
         ((2, 896, 256), BF),
         ((2, 4, 128, 256), BF),
-        ((2, 2, 128, 256), BF),
-        ((2, 2, 128, 256), BF),
+        ((2, 3, 128, 256), BF),
         ((2, 2, 128, 128), BF),
         ((2, 4, 128, 128), BF),
         ((2, D, SEQ), BF),
         ((D, SEQ), BF),
         ((2, D, SEQ), BF),
-        ((SEQ, D), BF),
+        ((SEQ, 512), BF),
         ((SEQ, 896), BF),
-        ((SEQ, 896), F32),
-        ((D, SEQ), F32),
+        ((4, SEQ, 1280), F32),
+        ((4, 512, SEQ), F32),
+        ((8, SEQ), F32),
         ((128, 128), F32),
         ((3, 2, Q, SEQ), BF),
         ((3, 2, Q, SEQ), BF),

time: 131 us -> 122 us (0.931)
  Pallas kernels: 128 us -> 120 us
    pallas_call x1, Pallas kernels: 128 us -> 120 us  [on_device(): pl.pallas_call(kernel, out_shape=jax.ShapeDtypeStruct((2, Q, SEQ), BF), i...]
where the time goes in v3:
time: 122 us
  Pallas kernels  120 us (98%)
  local copies, waits for them, and re-layouts  1.64 us (1%)
    pallas_call x1, Pallas kernels, on_device(): pl.pallas_call(kernel, out_shape=jax.ShapeDtypeStruct((2, Q, SEQ), BF), i...  120 us

profile of v3, /device:TPU:1, one launch (start us, length us, event | category | flops | bytes accessed | tf_op | source)
XLA Modules:
  0.0 121.9 jit_solution(14063282610753596907)
XLA Ops:
  0.7 119.6 %shard_map.145 = bf16[2,448,128]{2,1,0:T(8,128)(2,1)} custom-call(bf16[448,128]{1,0:T(8,128)(2,1)} %bitcast.32, bf16[448,128]{1,0:T(8,128)(2,1)} %bitcast.33, bf16[448,128]{1,0:T(8,128)(2,1)} %bitcast.34, bf16[1792,896]{1,0:T(8,128)(2,1)} %bitcast.25, bf16[1792,128]{1,0:T(8,128)(2,1)} %bitcast.30, bf16[14,1792]{1,0:T(8,128)(2,1)} %bitcast.35, ...), custom_call_target="tpu_custom_call" | custom-call | tf_op jit(solution)/shard_map/pallas_call | solution.py:848
  120.2 1.6 %copy.19 = bf16[2,1,128,448]{2,3,1,0:T(8,128)(2,1)} copy(bf16[2,1,128,448]{2,3,1,0:T(8,128)(2,1)} %bitcast.27) | data formatting | bytes 458752

commit v4 on v3

--- a/solution.py
+++ b/solution.py
@@ -42,7 +42,7 @@
     qkv_in, wo_ref, down_in, up_in, calls_ref,
     out_ref,
     xall, xs, wg, wr, rep, lane, wmix, wom, wom4, down, up, qw, a2s, a2r, ups, upr, low, misc,
-    acc, wog, wo32, mx, rs2s, rs2r, atb, atr, mid, hf, mbuf, ubuf, ybuf, xbuf, pbuf, sbuf, cbuf, rss,
+    acc, dbuf, cols, wog, wo32, mx, rs2s, rs2r, atb, atr, mid, hf, mbuf, ubuf, ybuf, xbuf, pbuf, sbuf, cbuf, rss,
     rsp, rsm,
     outq, send_sem, recv_sem, load_sem,
 ):
@@ -154,16 +154,6 @@
         shift = (width - (224 * i - first_tile)) % width
         return (pltpu.roll(window, shift, axis=1) if shift else window)[:, 0:256]
 
-    wo32[...] = jnp.zeros_like(wo32)
-    wo32[0:28, :] = wo_ref[...]
-    def owner(k):
-        return (k >= 56) * 1 + (k >= 112) * 1 + (k >= 168) * 1
-
-    k, c = iota((224, 64), 0), iota((224, 64), 1)
-    rep[...] = jnp.where(16 * owner(k) + ((k - 56 * owner(k)) & 15) == c, 1.0, 0.0).astype(BF)
-    k, c = iota((224, 128), 0), iota((224, 128), 1)
-    lane[...] = jnp.where((c >> 5) == ((k - 56 * owner(k)) >> 4), 1.0, 0.0).astype(BF)
-
     def tiles(query, keys, values):
         at = iota((query.shape[0], 128), 1)
         rest = values[:, 128:256]
@@ -212,6 +202,16 @@
     sends[("e1p",)] = x == 3
     pl.when(s == 63)(fresh.start)
     pl.when((x == 3) & (s != 63))(descs[("e1p",)].start)
+    wo32[...] = jnp.zeros_like(wo32)
+    wo32[0:28, :] = wo_ref[...]
+    def owner(k):
+        return (k >= 56) * 1 + (k >= 112) * 1 + (k >= 168) * 1
+
+    k, c = iota((224, 64), 0), iota((224, 64), 1)
+    rep[...] = jnp.where(16 * owner(k) + ((k - 56 * owner(k)) & 15) == c, 1.0, 0.0).astype(BF)
+    k, c = iota((224, 128), 0), iota((224, 128), 1)
+    lane[...] = jnp.where((c >> 5) == ((k - 56 * owner(k)) >> 4), 1.0, 0.0).astype(BF)
+
     a2r[x] = a2s[x]
     r, c = iota((224, 256), 0), iota((224, 256), 1)
     compact = jnp.where(((c - 8 * (c >> 6)) == r) & ((c & 63) < 56), 1.0, 0.0).astype(BF)
@@ -277,7 +277,6 @@
             push("down", 0, 3, "w0")
             here("up", 0, -2, "c0")
             here("up", 0, -2, "c1")
-            push("up", 0, -3, "w1")
             here("down", 0, 2, "c1")
             here("y", 0, 0, "c1")
         if step == 4:
@@ -288,6 +287,7 @@
         if step == 5:
             here("y", 0, -2, "w1")
             push("up", 1, -2, "w1")
+            push("up", 0, -3, "w1")
         if step == 6:
             here("y", 0, 2, "w1")
             push("down", 1, 2, "w1")
@@ -297,9 +297,10 @@
         if step == 8:
             here("down", 1, 2, "w0")
             push("down", 1, 3, "w0")
+            push("down", 0, 3, "o")
+        if step == 6.5:
             here("up", 1, -2, "w1")
             push("up", 1, -3, "w1")
-            push("down", 0, 3, "o")
         if step == 9:
             here("y", 0, 2, "o")
             push("down", 1, 2, "o")
@@ -564,22 +565,28 @@
         acc[n, :, 0:640] += dot(rows, wg[zz, yy, 0:224, :])
         acc[n, :, 640:768] += dot(rows, wr[zz, yy])
 
-    def attend(n):
+    def prepare(n):
         up_first = pick([upr[c] for c in range(3)], [m[:, 0:1] for m in marks_bf()])
         low_first = pick([low[c, n] for c in range(3)], marks_bf())
         scale_first = pick([misc[c, n, 0:1, :] for c in range(3)], marks())
+        dbuf[n, 0:128, :] = dot(low_first, up_first, TN)
+        dbuf[n, 128:256, :] = dot(low[3, n], upr[3], TN)
+        cols[n, 0:128, :] = jnp.broadcast_to(eye_column(scale_first, 128), (128, 128))
+        cols[n, 128:256, :] = jnp.broadcast_to(eye_column(misc[3, n, 0:1, :], 128), (128, 128))
+
+    def attend(n):
         causal = iota((128, 128), 0) >= iota((128, 128), 1)
         for slot in (0, 1):
-            low_t = low_first if slot == 0 else low[3, n]
-            up_slot = up_first if slot == 0 else upr[3]
-            scale = eye_column(scale_first if slot == 0 else misc[3, n, 0:1, :], 128)
             rows = slice(128 * slot, 128 * slot + 128)
-            total = acc[n, rows, :] * scale
-            rest = total[:, 640:768]
+            scale = cols[n, rows, :]
+            rest = acc[n, rows, 640:768] * scale
             rest = rest + pltpu.roll(rest, 64, axis=1)
             rest = rest + pltpu.roll(rest, 32, axis=1)
-            delta = dot(low_t, up_slot, TN)
-            proj = [total[:, 128 * t : 128 * t + 128] + delta[:, 128 * t : 128 * t + 128] for t in range(5)]
+            delta = dbuf[n, rows, :]
+            proj = [
+                acc[n, rows, 128 * t : 128 * t + 128] * scale + delta[:, 128 * t : 128 * t + 128]
+                for t in range(5)
+            ]
             proj.append(rest + delta[:, 640:768])
             at = iota((128, 128), 1)
             tail = jnp.where(
@@ -708,46 +715,51 @@
     pump(3)
     pump(4)
     line_first_pass()
+    pump(5)
     spread(0, (1,))
-    pump(5)
     for dz in (0, 1, -1, 2, -2):
         project(0, 0, dz)
     pump(6)
     line_first_share()
+    pass_got("h1p", state_rows(2))
+    pump(6.5)
     unpack(0, (0, 1, -1, 2, -2, 3, -3))
     unpack(1, (0, 1))
-    pass_got("h1p", state_rows(2))
+    project(0, 1, 0)
+    project(0, 1, 1)
+    pump(7)
+    pump(8)
     line_first_wait()
     spread(1, (1,))
-    pump(7)
-    pump(8)
-    project(0, 1, 0)
-    project(0, 1, 1)
     pass_wait("h1p")
     line_start(2)
+    project(0, 1, 2)
+    project(0, 1, -2)
     make_low(1)
+    up_wait()
+    prepare(0)
     here("down", 0, 3, "w0")
     here("up", 0, -3, "w1")
     project(0, 0, 3)
     project(0, 0, -3)
     project(0, 0, 4)
     here("down", 1, 2, "w1")
-    here("up", 1, -2, "w0")
-    for dz in (2, -2, 3, -3):
-        project(0, 1, dz)
+    project(0, 1, 3)
     here("y", 0, -1, "w1")
     here("up", 1, 0, "w0")
     project(0, 1, -1)
+    here("up", 1, -2, "w0")
+    project(0, 1, -3)
     here("down", 1, 3, "w0")
     here("up", 1, -3, "w1")
     project(0, 1, 4)
-    up_wait()
     pump(9)
     attend(0)
     send_mixed(0)
+    project_rest(8, 12)
     pump(10)
     line_pass(2)
-    project_rest(8, 16)
+    project_rest(12, 16)
     pump(11)
     unpack(0, (4,))
     unpack(1, (-1, 2, -2, 3, -3, 4))
@@ -758,6 +770,7 @@
     spread(1, (0,))
     send_attn(0)
     project_rest(0, 8)
+    prepare(1)
     attend(1)
     send_mixed(1)
     make_middle(0)
@@ -824,6 +837,8 @@
         ((4, 2, 128, 128), BF),
         ((4, 2, 8, 128), F32),
         ((2, 256, 768), F32),
+        ((2, 256, 768), F32),
+        ((2, 256, 128), F32),
         ((512, 896), BF),
         ((32, 896), BF),
         ((2, 896, 256), BF),

time: 122 us -> 120 us (0.984)
  Pallas kernels: 120 us -> 118 us
    pallas_call x1, Pallas kernels: 120 us -> 118 us  [on_device(): pl.pallas_call(kernel, out_shape=jax.ShapeDtypeStruct((2, Q, SEQ), BF), i...]
where the time goes in v4:
time: 120 us
  Pallas kernels  118 us (98%)
  local copies, waits for them, and re-layouts  1.64 us (1%)
    pallas_call x1, Pallas kernels, on_device(): pl.pallas_call(kernel, out_shape=jax.ShapeDtypeStruct((2, Q, SEQ), BF), i...  118 us

profile of v4, /device:TPU:1, one launch (start us, length us, event | category | flops | bytes accessed | tf_op | source)
XLA Modules:
  0.0 120.0 jit_solution(11830243990074177185)
XLA Ops:
  0.7 117.7 %shard_map.145 = bf16[2,448,128]{2,1,0:T(8,128)(2,1)} custom-call(bf16[448,128]{1,0:T(8,128)(2,1)} %bitcast.32, bf16[448,128]{1,0:T(8,128)(2,1)} %bitcast.33, bf16[448,128]{1,0:T(8,128)(2,1)} %bitcast.34, bf16[1792,896]{1,0:T(8,128)(2,1)} %bitcast.25, bf16[1792,128]{1,0:T(8,128)(2,1)} %bitcast.30, bf16[14,1792]{1,0:T(8,128)(2,1)} %bitcast.35, ...), custom_call_target="tpu_custom_call" | custom-call | tf_op jit(solution)/shard_map/pallas_call | solution.py:863
  118.4 1.6 %copy.19 = bf16[2,1,128,448]{2,3,1,0:T(8,128)(2,1)} copy(bf16[2,1,128,448]{2,3,1,0:T(8,128)(2,1)} %bitcast.27) | data formatting | bytes 458752
